TPU v7x, 256 devices: a whole 4x4x8 slice. The times are simulated.
256 devices in a mesh: kvh: 8 (over y, core), seq: 32 (over x, z).
Axes of the slice: x: 4, y: 4, z: 8, core: 2. Of those that a mesh axis runs over, the one named last changes fastest.
Arguments:
- queries: bfloat16 [16, 128, 128], P(None, 'kvh'), may hold values from -20 to 20
- token_keys: bfloat16 [16, 8, 128], P(None, 'kvh'), may hold values from -6 to 6
- token_values: bfloat16 [16, 8, 128], P(None, 'kvh'), may hold values from -6 to 6
- key_cache: bfloat16 [16, 4096, 8, 128], P(None, 'seq', 'kvh'), may hold values from -20 to 20
- cached_value_rows: bfloat16 [16, 4096, 8, 128], P(None, 'seq', 'kvh'), may hold values from -6 to 6
- lengths: int32 [16], replicated, may hold values from 1024 to 4096, as said below
- residual: bfloat16 [16, 16384], P(None, 'seq'), may hold values from -7 to 7
- out_weight: bfloat16 [16384, 16384], P('kvh', 'seq'), may hold values from -0.1875 to 0.1875
- norm_gain: bfloat16 [16384], P('seq'), may hold values from 0.099609375 to 1.8984375
- gate_weight: bfloat16 [16384, 26624], P('seq', 'kvh'), may hold values from -0.046875 to 0.046875
- up_weight: bfloat16 [16384, 26624], P('seq', 'kvh'), may hold values from -0.046875 to 0.046875
- down_weight: bfloat16 [26624, 16384], P('kvh', 'seq'), may hold values from -0.0390625 to 0.0390625
Outputs:
- updated: bfloat16 [16, 16384], P(None, 'seq')
- attended: bfloat16 [16, 16384], P(None, 'kvh')
Inputs may be any that keep to these rules, and one draw needn't show every extreme that they name: Each request's cached tokens fill slots 0 to lengths - 1; some request has exactly 4096 and some exactly 1024.
All inputs are finite; a program needn't handle non-finite values.
Results may differ from a plain program's by a relative error of at most 0.008.
Values may be sent and summed in bfloat16 or wider, within the bound.
No kernel may reach another device: no remote copies, remote signals or barrier semaphores. Data moves between devices by JAX's collectives and lax.ppermute only.
A program may use at most 64 MiB of HBM per device.

v0:
```python
import jax
import jax.numpy as jnp
from jax import lax
from jax.sharding import PartitionSpec as P

D = 16384


def merged(value, axis, combine):
    everything = jax.tree.map(lambda part: lax.all_gather(part, axis), value)
    initial = jax.tree.map(lambda part: part[0], everything)

    def hop(k, so_far):
        return combine(so_far, jax.tree.map(lambda part: part[k], everything))

    return lax.fori_loop(1, lax.axis_size(axis), hop, initial)


def combine(first_part, second_part):
    first_peak, first_total, first_acc = first_part
    second_peak, second_total, second_acc = second_part
    new_peak = jnp.maximum(first_peak, second_peak)
    first_factor = jnp.exp(first_peak - new_peak)
    second_factor = jnp.exp(second_peak - new_peak)
    total_sum = first_total * first_factor + second_total * second_factor
    accumulated = first_acc * first_factor[..., None] + second_acc * second_factor[..., None]
    return (new_peak, total_sum, accumulated)


def shards(
    queries,
    token_keys,
    token_values,
    key_cache,
    cached_value_rows,
    lengths,
    residual,
    out_weight,
    norm_gain,
    gate_weight,
    up_weight,
    down_weight,
):
    requests, local_heads, head_size = queries.shape
    slot_count = key_cache.shape[1]
    kv_local = key_cache.shape[2]
    query_groups = local_heads // kv_local
    score_scale = head_size ** (-0.5)
    query_input = queries.reshape(requests, kv_local, query_groups, head_size)
    scores = (
        jnp.einsum("bkgd,bskd->bkgs", query_input, key_cache, preferred_element_type=jnp.float32)
        * score_scale
    )
    first_slot = lax.axis_index("seq") * slot_count
    is_valid = (first_slot + jnp.arange(slot_count))[None, :] < lengths[:, None]
    is_valid = is_valid[:, None, None, :]
    is_owner = lax.axis_index("seq") == 0
    fresh_score = (
        jnp.einsum("ctei,cti->cte", query_input, token_keys, preferred_element_type=jnp.float32)
        * score_scale
    )
    fresh_score = jnp.where(is_owner, fresh_score, -1e30)
    scores = jnp.where(is_valid, scores, -1e30)
    row_peak = jnp.maximum(jnp.max(scores, -1), fresh_score)
    weights = jnp.where(is_valid, jnp.exp(scores - row_peak[..., None]), 0.0)
    own_weight = jnp.where(is_owner, jnp.exp(fresh_score - row_peak), 0.0)
    total_sum = jnp.sum(weights, -1) + own_weight
    rounded = weights.astype(jnp.bfloat16)
    own_rounded = lax.optimization_barrier(own_weight.astype(jnp.bfloat16)).astype(jnp.float32)
    accumulated = jnp.einsum(
        "bkgs,bskd->bkgd", rounded, cached_value_rows, preferred_element_type=jnp.float32
    )
    accumulated = (
        accumulated + own_rounded[..., None] * token_values.astype(jnp.float32)[:, :, None, :]
    )
    merged_peak, merged_total, merged_acc = merged(
        (row_peak, total_sum, accumulated), "seq", combine
    )
    attended = (
        (merged_acc / merged_total[..., None])
        .astype(jnp.bfloat16)
        .reshape(requests, local_heads * head_size)
    )
    projected = jnp.dot(attended, out_weight, preferred_element_type=jnp.float32)
    projected = lax.psum(projected, "kvh")
    middle = (residual.astype(jnp.float32) + projected).astype(jnp.bfloat16)
    wide = middle.astype(jnp.float32)
    square_sum = lax.psum(jnp.sum(wide * wide, -1), "seq")
    inverse = lax.rsqrt(square_sum / D + 1e-05)
    normed = (wide * inverse[:, None] * norm_gain.astype(jnp.float32)).astype(jnp.bfloat16)
    gate_proj = jnp.dot(normed, gate_weight, preferred_element_type=jnp.float32)
    up_proj = jnp.dot(normed, up_weight, preferred_element_type=jnp.float32)
    gate_proj, up_proj = lax.psum((gate_proj, up_proj), "seq")
    hidden = (jax.nn.silu(gate_proj) * up_proj).astype(jnp.bfloat16)
    down_proj = jnp.dot(hidden, down_weight, preferred_element_type=jnp.float32)
    down_proj = lax.psum(down_proj, "kvh")
    updated = (wide + down_proj).astype(jnp.bfloat16)
    return (updated, attended)


def solution(mesh):
    return jax.shard_map(
        shards,
        mesh=mesh,
        in_specs=(
            P(None, "kvh", None),
            P(None, "kvh", None),
            P(None, "kvh", None),
            P(None, "seq", "kvh", None),
            P(None, "seq", "kvh", None),
            P(),
            P(None, "seq"),
            P("kvh", "seq"),
            P("seq"),
            P("seq", "kvh"),
            P("seq", "kvh"),
            P("kvh", "seq"),
        ),
        out_specs=(P(None, "seq"), P(None, "kvh")),
        check_vma=False,
    )
```

profile of v0, /device:TPU:1, one launch (start us, length us, event | category | flops | bytes accessed | tf_op | source)
XLA Modules:
  0.0 446.6 jit_solution(8891359524790326387)
XLA Ops:
  7.2 0.9 broadcast_compare_fusion
  8.1 1.1 fusion.16
  9.2 1.6 fusion.26
  11.7 2.0 convolution_add_fusion
  13.8 41.2 %all-gather.1 = f32[512,16]{1,0:T(8,128)S(1)} all-gather(f32[16,16]{1,0:T(8,128)S(1)} %get-tuple-element.220), channel_id=3, replica_groups=mesh['kvh'=8,'seq'=32] {'seq'}, dimensions={0}, use_global_device_ids=true | all-gather | bytes 33792 | tf_op jit(solution)/shard_map/all_gather | solution.py:10
  55.7 40.5 %all-gather = f32[512,16]{1,0:T(8,128)S(1)} all-gather(f32[16,16]{1,0:T(8,128)S(1)} %fusion.18), channel_id=2, replica_groups=mesh['kvh'=8,'seq'=32] {'seq'}, dimensions={0}, use_global_device_ids=true | all-gather | bytes 33792 | tf_op jit(solution)/shard_map/all_gather | solution.py:10
  96.9 1.3 convert_element_type.43
  98.2 0.9 slice_bitcast_fusion
  99.1 56.9 %while.19 = (s32[]{:T(128)}, f32[16,1,16]{2,1,0:T(1,128)S(1)}, f32[16,1,16]{2,1,0:T(1,128)S(1)}, f32[16,1,16,128]{3,2,1,0:T(8,128)S(1)}, f32[32,16,1,16]{3,1,2,0...) while((s32[]{:T(128)}, f32[16,1,16]{2,1,0:T(1,128)S(1)}, ...), condition=%wide.region_3.4_spmd, body=%wide.region_2.3_spmd.sunk | while | flops 99845 | bytes 407703 | solution.py:16
  99.9 1.1 fusion.36
  101.0 0.7 constant_dynamic-slice_fusion.3
  101.7 1.1 fusion.36
  103.5 1.1 fusion.36
  104.6 0.7 constant_dynamic-slice_fusion.3
  105.4 1.1 fusion.36
  107.2 1.1 fusion.36
  108.3 0.7 constant_dynamic-slice_fusion.3
  109.0 1.1 fusion.36
  110.9 1.1 fusion.36
  112.0 0.7 constant_dynamic-slice_fusion.3
  112.7 1.1 fusion.36
  113.8 0.7 constant_dynamic-slice_fusion.3
  114.5 1.1 fusion.36
  115.6 0.7 constant_dynamic-slice_fusion.3
  116.4 1.1 fusion.36
  118.2 1.1 fusion.36
  119.3 0.7 constant_dynamic-slice_fusion.3
  120.1 1.1 fusion.36
  121.9 1.1 fusion.36
  123.0 0.7 constant_dynamic-slice_fusion.3
  123.7 1.1 fusion.36
  124.8 0.7 constant_dynamic-slice_fusion.3
  125.6 1.1 fusion.36
  127.4 1.1 fusion.36
  128.5 0.7 constant_dynamic-slice_fusion.3
  129.2 1.1 fusion.36
  131.1 1.1 fusion.36
  132.2 0.7 constant_dynamic-slice_fusion.3
  132.9 1.1 fusion.36
  134.7 1.1 fusion.36
  135.8 0.7 constant_dynamic-slice_fusion.3
  136.6 1.1 fusion.36
  138.4 1.1 fusion.36
  139.5 0.7 constant_dynamic-slice_fusion.3
  140.2 1.1 fusion.36
  141.3 0.7 constant_dynamic-slice_fusion.3
  142.1 1.1 fusion.36
  143.9 1.1 fusion.36
  145.0 0.7 constant_dynamic-slice_fusion.3
  145.7 1.1 fusion.36
  147.6 1.1 fusion.36
  149.4 1.1 fusion.36
  151.3 1.1 fusion.36
  153.1 1.1 fusion.36
  154.9 1.1 fusion.36
  156.2 2.0 fusion.27
  158.1 40.2 %psum.35 = f32[16,512]{1,0:T(8,128)S(1)} all-reduce(f32[16,512]{1,0:T(8,128)S(1)} %fusion.27), channel_id=1, replica_groups=mesh['kvh'=8,'seq'=32] {'kvh'}, use_global_device_ids=true, to_apply=%region_4.5 | all-reduce | flops 8192 | bytes 65536 | tf_op jit(solution)/shard_map/psum | solution.py:85
  198.3 0.8 fusion.12
  199.2 58.4 %psum.36 = f32[16]{0:T(128)S(1)} all-reduce(f32[16]{0:T(128)S(1)} %get-tuple-element.215), channel_id=1, replica_groups=mesh['kvh'=8,'seq'=32] {'seq'}, use_global_device_ids=true, to_apply=%region_6.7 | all-reduce | flops 16 | bytes 128 | tf_op jit(solution)/shard_map/psum | solution.py:88
  257.6 2.1 fusion.21
  259.7 1.3 fusion.19
  261.0 150.3 %all-reduce.3.cloned.1.call-done = (f32[16,3328]{1,0:T(8,128)}, f32[16,3328]{1,0:T(8,128)}) async-done(((f32[16,3328]{1,0:T(8,128)}, f32[16,3328]{1,0:T(8,128)}), (f32[16,3328]{1,0:T(8,128)}, f32[16,3328]{1,0:T(8,128)})) %all-reduce.3.cloned.1.call-update) | async-done | bytes 426000 | tf_op jit(solution)/shard_map/psum | solution.py:93
  411.3 2.7 fusion.6
  414.0 25.1 %psum.39 = f32[16,512]{1,0:T(8,128)S(1)} all-reduce(f32[16,512]{1,0:T(8,128)S(1)} %fusion.6), channel_id=1, replica_groups=mesh['kvh'=8,'seq'=32] {'kvh'}, use_global_device_ids=true, to_apply=%region_9.10 | all-reduce | flops 8192 | bytes 65536 | tf_op jit(solution)/shard_map/psum | solution.py:96
  (76 shorter events, 15.2 us)
Async XLA Ops:
  7.2 250.4 %copy-start = (bf16[512,3328]{1,0:T(8,128)(2,1)S(1)}, bf16[512,3328]{1,0:T(8,128)(2,1)}, u32[]{:S(2)}) copy-start(bf16[512,3328]{1,0:T(8,128)(2,1)} %param.23) | copy-start | bytes 10223620
  7.2 91.0 %all-gather.5.cloned.1.call-start = ((), (), s32[]{:S(2)}) async-start(), calls=%async_computation | async-start | bytes 4325376 | tf_op jit(solution)/shard_map/all_gather | solution.py:10
  13.7 397.6 %all-reduce.3.cloned.1.call-start = ((), (), s32[]{:S(2)}) async-start(), calls=%async_computation.1 | async-start | bytes 851968 | tf_op jit(solution)/shard_map/psum | solution.py:93
  55.0 0.7 copy-start.2
  96.2 0.7 copy-start.3
  156.1 104.9 %copy-start.4 = (bf16[2,8,16,128]{3,1,2,0:T(8,128)(2,1)}, bf16[2,8,16,128]{3,1,2,0:T(8,128)(2,1)S(1)}, u32[]{:S(2)}) copy-start(bf16[2,8,16,128]{3,1,2,0:T(8,128)(2,1)S(1)} %copy.24) | copy-start | bytes 196612
  198.3 61.4 %copy-start.5 = (f32[512]{0:T(512)S(1)}, f32[512]{0:T(512)}, u32[]{:S(2)}) copy-start(f32[512]{0:T(512)} %convert_element_type.43) | copy-start | bytes 6148
  257.6 2.1 copy-start.1
Sparse Core Ops, SparseCore 0:
  13.8 83.4 all-gather.4
  261.2 150.1 all-reduce.2
where the time goes:
time: 452 us; the launch traced here: 447 us
  blocking collectives  205 us (45%)
  waiting for transfers between devices  150 us (33%)
  other arithmetic  38.3 us (8%)
  local copies, waits for them, and re-layouts  24.7 us (5%)
  between operations  14.2 us (3%)
  matrix products  12.7 us (3%)
    psum x1, waiting for transfers between devices, shards(): gate_proj, up_proj = lax.psum((gate_proj, up_proj), 'seq')  150 us
    all_gather x2, blocking collectives, merged(): everything = jax.tree.map(lambda part: lax.all_gather(part, axis), value)  81.8 us
    psum x1, blocking collectives, shards(): square_sum = lax.psum(jnp.sum(wide * wide, -1), 'seq')  58.4 us
    psum x1, blocking collectives, shards(): projected = lax.psum(projected, 'kvh')  40.2 us
    add x31, other arithmetic, combine(): first_acc * first_factor[..., None] + second_acc * second_factor[..., None]  33.3 us
    psum x1, blocking collectives, shards(): down_proj = lax.psum(down_proj, 'kvh')  25.1 us
    dynamic_slice x31, local copies, waits for them, and re-layouts, hop(): return combine(so_far, jax.tree.map(lambda part: part[k], everything))  22.4 us
  transfers between devices with their start and end apart: 2, of which 1 were waited for; matrix products, arithmetic and copies ran while one was open for 0% of the time, Pallas kernels for 0%

commit v1 on v0

v1 whole, which is shorter than its diff:
```python
import jax
import jax.numpy as jnp
from jax import lax
from jax.experimental import pallas as pl
from jax.experimental.pallas import tpu as pltpu
from jax.sharding import PartitionSpec as P

D = 16384
BF = jnp.bfloat16
F32 = jnp.float32
LANES = 128
MIB = 1 << 20
KEY_PARTS = 4
VMEM = pl.BlockSpec(memory_space=pltpu.VMEM)
SMEM = pl.BlockSpec(memory_space=pltpu.SMEM)
HBM = pl.BlockSpec(memory_space=pltpu.HBM)
DMA = pltpu.SemaphoreType.DMA


def call(body, out_shape, n_in, scratch=(), smem=(), hbm=(), limit=16 * MIB):
    kernel = pl.pallas_call(
        body,
        out_shape=out_shape,
        in_specs=[SMEM if i in smem else HBM if i in hbm else VMEM for i in range(n_in)],
        out_specs=jax.tree.map(lambda _: VMEM, out_shape),
        scratch_shapes=list(scratch),
        compiler_params=pltpu.CompilerParams(vmem_limit_bytes=limit),
    )

    def run(*args):
        return kernel(
            *[
                pltpu.with_memory_space_constraint(arg, pltpu.HBM) if i in hbm else arg
                for i, arg in enumerate(args)
            ]
        )

    return run


def bf(*shape):
    return jax.ShapeDtypeStruct(shape, BF)


def round_bf(value):
    return value.astype(BF).astype(F32)


def lane_index(shape):
    return lax.broadcasted_iota(jnp.int32, shape, len(shape) - 1)


def stat_rows(columns):
    rows = columns[0].shape[0]
    lane = lane_index((rows, LANES))
    out = jnp.zeros((rows, LANES), F32)
    for index, column in enumerate(columns):
        out = jnp.where(lane == index, column, out)
    return out


def two_parts(value):
    high = round_bf(value)
    return high, value - high


def start_copies(sources, targets, sems):
    copies = [
        pltpu.make_async_copy(source, target, sems.at[i])
        for i, (source, target) in enumerate(zip(sources, targets))
    ]
    for copy in copies:
        copy.start()
    return copies


def attention_kernel(where_ref, *refs):
    sources, refs = refs[:8], refs[-12:]
    out_ref, kept_ref, row_ref = refs[:3]
    targets, sems = refs[3:11], refs[11]
    len_ref, q_ref, tk_ref, k_ref, tv_ref, v_ref, res_ref, gn_ref = targets
    chunk = k_ref.shape[0] // KEY_PARTS
    chunks = [pl.ds(i * chunk, chunk) for i in range(KEY_PARTS)]
    copies = start_copies(
        [*sources[:3], *(sources[3].at[c] for c in chunks), *sources[4:]],
        [*targets[:3], *(targets[3].at[c] for c in chunks), *targets[4:]],
        sems,
    )
    for copy in copies[:3]:
        copy.wait()
    keys, others = copies[3 : 3 + KEY_PARTS], copies[3 + KEY_PARTS :]
    requests, heads, size = q_ref.shape
    slots = k_ref.shape[1]
    scale = size ** (-0.5)
    first = where_ref[0] * slots
    owner = where_ref[0] == 0
    contract = (((1,), (1,)), ((), ()))
    slot = first + lane_index((heads, slots))
    scores, valid, fresh = [], [], []
    for b in range(requests):
        if b % chunk == 0:
            keys[b // chunk].wait()
        q = q_ref[b]
        scores.append(lax.dot_general(q, k_ref[b], contract, preferred_element_type=F32))
        valid.append(jnp.where(slot < len_ref[b], 1.0, 0.0))
        fresh.append(q.astype(F32) * tk_ref[b : b + 1, :].astype(F32))
    valid = jnp.concatenate(valid, 0) > 0.5
    scores = jnp.where(valid, jnp.concatenate(scores, 0) * scale, -1e30)
    fresh = jnp.sum(jnp.concatenate(fresh, 0), -1, keepdims=True) * scale
    fresh = jnp.where(owner, fresh, -1e30)
    peak = round_bf(jnp.maximum(jnp.max(scores, -1, keepdims=True), fresh))
    weights = jnp.where(valid, jnp.exp(scores - peak), 0.0)
    own = jnp.where(owner, jnp.exp(fresh - peak), 0.0)
    total = jnp.sum(weights, -1, keepdims=True) + own
    rounded = weights.astype(BF)
    own = round_bf(own)
    stats = stat_rows((peak,) + two_parts(total)).astype(BF)
    for copy in others:
        copy.wait()
    for b in range(requests):
        rows = slice(b * heads, (b + 1) * heads)
        acc = jnp.dot(rounded[rows], v_ref[b], preferred_element_type=F32)
        acc = acc + own[rows] * tv_ref[b : b + 1, :].astype(F32)
        out_ref[b, :, :size] = acc.astype(BF)
        out_ref[b, :, size:] = stats[rows]
    kept_ref[...] = res_ref[...]
    gain = gn_ref[...].astype(F32)
    row_ref[...] = jnp.concatenate([gain[i : i + 1] for i in range(gain.shape[0])], -1)


def merge_kernel(got_ref, out_ref):
    size = out_ref.shape[-1]
    stats = got_ref[:, :, size:].astype(F32)
    peak = stats[:, :, 0:1]
    factor = jnp.exp(peak - jnp.max(peak, 0, keepdims=True))
    total = jnp.sum((stats[:, :, 1:2] + stats[:, :, 2:3]) * factor, 0)
    acc = jnp.sum(got_ref[:, :, :size].astype(F32) * factor, 0)
    out_ref[...] = jnp.broadcast_to((acc / total).astype(BF)[None], out_ref.shape)


def project_kernel(got_ref, weight_ref, attended_ref, out_ref, rows_ref):
    requests = attended_ref.shape[0]
    heads = rows_ref.shape[0] // requests
    rows_ref[...] = got_ref[...].astype(F32).reshape(rows_ref.shape)
    attended = jnp.concatenate(
        [rows_ref[pl.ds(h, requests, stride=heads), :].astype(BF) for h in range(heads)], -1
    )
    attended_ref[...] = attended
    projected = jnp.dot(attended, weight_ref[...], preferred_element_type=F32)
    out_ref[...] = jnp.broadcast_to(projected.astype(BF)[None], out_ref.shape)


def gate_up_kernel(
    got_ref, residual_ref, gain_ref, gate_ref, up_ref, middle_ref, out_ref, rows_ref
):
    pieces, depth, _ = out_ref.shape
    requests = residual_ref.shape[0]
    halves = pieces // requests
    projected = jnp.sum(got_ref[...].astype(F32), 0)
    middle = (residual_ref[...].astype(F32) + projected).astype(BF)
    middle_ref[...] = middle
    middle = middle.astype(F32)
    square = jnp.sum(middle * middle, -1, keepdims=True)
    scaled = (middle * gain_ref[...]).astype(BF)
    blocks = gate_ref.shape[1] // (halves * LANES)

    def put(row, half, value):
        rows_ref[pl.ds(half * depth + row, requests, stride=halves * depth), :] = value

    for start, weight_ref in ((0, gate_ref), (blocks, up_ref)):
        product = jnp.dot(scaled, weight_ref[...], preferred_element_type=F32)
        for j in range(halves * blocks):
            put(start + j % blocks, j // blocks, product[:, j * LANES : (j + 1) * LANES])
    stats = stat_rows(two_parts(square))
    zeros = jnp.zeros_like(stats)
    for half in range(halves):
        put(2 * blocks, half, stats)
        for row in range(2 * blocks + 1, depth):
            put(row, half, zeros)
    out_ref[...] = rows_ref[...].astype(BF).reshape(out_ref.shape)


def hidden_kernel(blocks, got_ref, out_ref):
    summed = jnp.sum(got_ref[...].astype(F32), 0)
    stats = summed[2 * blocks : 2 * blocks + 1]
    square = stats[:, 0:1] + stats[:, 1:2]
    inverse = lax.rsqrt(square / D + 1e-05)
    gate = summed[:blocks] * inverse
    up = summed[blocks : 2 * blocks] * inverse
    hidden = gate / (1.0 + jnp.exp(-gate)) * up
    pad = jnp.zeros((out_ref.shape[1] - blocks, LANES), F32)
    hidden = jnp.concatenate([hidden, pad], 0).astype(BF)
    out_ref[...] = jnp.broadcast_to(hidden[None], out_ref.shape)


def down_kernel(got_ref, weight_ref, out_ref, rows_ref):
    pieces, depth, _ = got_ref.shape
    requests = out_ref.shape[1]
    halves = pieces // requests
    blocks = weight_ref.shape[0] // (halves * LANES)
    rows_ref[...] = got_ref[...].astype(F32).reshape(rows_ref.shape)
    hidden = jnp.concatenate(
        [
            rows_ref[pl.ds(half * depth + row, requests, stride=halves * depth), :].astype(BF)
            for half in range(halves)
            for row in range(blocks)
        ],
        -1,
    )
    down = jnp.dot(hidden, weight_ref[...], preferred_element_type=F32)
    out_ref[...] = jnp.broadcast_to(down.astype(BF)[None], out_ref.shape)


def finish_kernel(got_ref, middle_ref, out_ref):
    down = jnp.sum(got_ref[...].astype(F32), 0)
    out_ref[...] = (middle_ref[...].astype(F32) + down).astype(BF)


def exchange(pieces, axis):
    return lax.all_to_all(pieces, axis, 0, 0)


def shards(
    queries,
    token_keys,
    token_values,
    key_cache,
    cached_value_rows,
    lengths,
    residual,
    out_weight,
    norm_gain,
    gate_weight,
    up_weight,
    down_weight,
):
    requests, heads, size = queries.shape
    seq, kvh = lax.axis_size("seq"), lax.axis_size("kvh")
    rows = requests * heads // seq
    width = residual.shape[1]
    halves = seq // requests
    blocks = gate_weight.shape[1] // (halves * LANES)
    depth = -(-(2 * blocks + 1) // 16) * 16
    thin = -(-blocks // 16) * 16
    where = lax.axis_index("seq").reshape(1)

    cache = (requests, key_cache.shape[1], size)
    packed, residual, gain = call(
        attention_kernel,
        (
            bf(requests, heads, 2 * size),
            bf(requests, width),
            jax.ShapeDtypeStruct((1, width), F32),
        ),
        12,
        scratch=[
            pltpu.SMEM((requests,), jnp.int32),
            pltpu.VMEM((requests, heads, size), BF),
            pltpu.VMEM((requests, size), BF),
            pltpu.VMEM(cache, BF),
            pltpu.VMEM((requests, size), BF),
            pltpu.VMEM(cache, BF),
            pltpu.VMEM((requests, width), BF),
            pltpu.VMEM((width // LANES, LANES), BF),
            DMA((7 + KEY_PARTS,)),
        ],
        smem=(0,),
        hbm=range(1, 12),
    )(
        where,
        lengths,
        queries,
        token_keys.reshape(requests, size),
        key_cache.reshape(cache),
        token_values.reshape(requests, size),
        cached_value_rows.reshape(cache),
        residual,
        norm_gain.reshape(-1, LANES),
        gate_weight,
        up_weight,
        down_weight,
    )
    got = exchange(packed.reshape(seq, rows, 2 * size), "seq")
    merged = call(merge_kernel, bf(seq, rows, size), 1)(got)
    attended, projected = call(
        project_kernel,
        (bf(requests, heads * size), bf(kvh, requests, width)),
        2,
        scratch=[pltpu.VMEM((requests * heads, size), F32)],
    )(exchange(merged, "seq"), out_weight)
    middle, pieces = call(
        gate_up_kernel,
        (bf(requests, width), bf(seq, depth, LANES)),
        5,
        scratch=[
            pltpu.VMEM((seq * depth, LANES), F32),
        ],
    )(exchange(projected, "kvh"), residual, gain, gate_weight, up_weight)
    hidden = call(lambda *refs: hidden_kernel(blocks, *refs), bf(seq, thin, LANES), 1)(
        exchange(pieces, "seq")
    )
    down = call(
        down_kernel,
        bf(kvh, requests, width),
        2,
        scratch=[pltpu.VMEM((seq * thin, LANES), F32)],
    )(exchange(hidden, "seq"), down_weight)
    updated = call(finish_kernel, bf(requests, width), 2)(exchange(down, "kvh"), middle)
    return (updated, attended)


def solution(mesh):
    return jax.shard_map(
        shards,
        mesh=mesh,
        in_specs=(
            P(None, "kvh", None),
            P(None, "kvh", None),
            P(None, "kvh", None),
            P(None, "seq", "kvh", None),
            P(None, "seq", "kvh", None),
            P(),
            P(None, "seq"),
            P("kvh", "seq"),
            P("seq"),
            P("seq", "kvh"),
            P("seq", "kvh"),
            P("kvh", "seq"),
        ),
        out_specs=(P(None, "seq"), P(None, "kvh")),
        check_vma=False,
    )
```

time: 452 us -> 91.7 us (0.20); the launches traced: 447 us -> 91.5 us
  waiting for transfers between devices: 150 us -> 0 us
  blocking collectives: 205 us -> 84.7 us
  other arithmetic: 38.3 us -> 0 us
  local copies, waits for them, and re-layouts: 24.7 us -> 0.02 us
  between operations: 14.2 us -> 0.7 us
  matrix products: 12.7 us -> 0 us
  Pallas kernels: 0 us -> 5.98 us
    psum x1 -> x0, waiting for transfers between devices: 150 us -> none  [shards(): gate_proj, up_proj = lax.psum((gate_proj, up_proj), 'seq')]
    psum x3 -> x0, blocking collectives: 124 us -> none  [the longest x1 58.4 us: shards(): square_sum = lax.psum(jnp.sum(wide * wide, -1), 'seq')]
    all_to_all x0 -> x6, blocking collectives: none -> 84.7 us  [exchange(): return lax.all_to_all(pieces, axis, 0, 0)]
    all_gather x2 -> x0, blocking collectives: 81.8 us -> none  [merged(): everything = jax.tree.map(lambda part: lax.all_gather(part, axis), value)]
    add x63 -> x0, other arithmetic: 33.7 us -> none  [the longest x31 33.3 us: combine(): first_acc * first_factor[..., None] + second_acc * second_factor[..., None]]
    dynamic_slice x31 -> x0, local copies, waits for them, and re-layouts: 22.4 us -> none  [hop(): return combine(so_far, jax.tree.map(lambda part: part[k], everything))]
    dot_general x7 -> x0, matrix products: 12.7 us -> none  [the longest x1 2.73 us: shards(): down_proj = jnp.dot(hidden, down_weight, preferred_element_type=jnp.float32)]
    pallas_call x0 -> x7, Pallas kernels: none -> 5.98 us  [run(): kernel(*[pltpu.with_memory_space_constraint(arg, pltpu.HBM) if i in hbm e...]
  transfers between devices with their start and end apart: 2 -> 0, of which waited for: 1 -> 0; matrix products, arithmetic and copies ran while one was open for 0% -> 0% of each run, Pallas kernels for 0% -> 0%
where the time goes in v1:
time: 91.7 us; the launch traced here: 91.5 us
  blocking collectives  84.7 us (92%)
  Pallas kernels  5.98 us (7%)
    all_to_all x6, blocking collectives, exchange(): return lax.all_to_all(pieces, axis, 0, 0)  84.7 us
    pallas_call x7, Pallas kernels, run(): kernel(*[pltpu.with_memory_space_constraint(arg, pltpu.HBM) if i in hbm e...  5.98 us

profile of v1, /device:TPU:1, one launch (start us, length us, event | category | flops | bytes accessed | tf_op | source)
XLA Modules:
  0.0 91.5 jit_solution(13942322479619499244)
XLA Ops:
  0.6 0.0 copy-start.3
  0.6 0.0 copy-start
  0.7 0.0 copy-start.1
  0.7 2.4 %shard_map.131 = (bf16[16,16,256]{2,1,0:T(8,128)(2,1)S(1)}, bf16[16,512]{1,0:T(8,128)(2,1)S(1)}, f32[1,512]{1,0:T(1,128)S(1)}) custom-call(s32[1]{0:T(128)} %bitcast.where_ref, s32[16]{0:T(128)} %refs_0_.1, bf16[16,16,128]{2,1,0:T(8,128)(2,1)} %refs_1_.1, bf16[16,128]{1,0:T(8,128)(2,1)} %bitcast.10, bf16[16,128,128]{2,1,0:T(8,128)(2,1)} %bitcast.8, ...), custom_call_target="tpu_custom_call" | custom-call | tf_op jit(solution)/shard_map/pallas_call | solution.py:31
  3.0 20.9 %all_to_all.30.got_ref = bf16[32,8,256]{2,1,0:T(8,128)(2,1)S(1)} all-to-all(bf16[32,8,256]{2,1,0:T(8,128)(2,1)S(1)} %bitcast.7), channel_id=1, replica_groups=mesh['kvh'=8,'seq'=32] {'seq'}, dimensions={0} | all-to-all | bytes 262144 | tf_op jit(solution)/shard_map/all_to_all | solution.py:220
  24.0 0.2 shard_map.132
  24.2 12.4 %all_to_all.31.got_ref = bf16[32,8,128]{2,1,0:T(8,128)(2,1)S(1)} all-to-all(bf16[32,8,128]{2,1,0:T(8,128)(2,1)S(1)} %shard_map.132), channel_id=1, replica_groups=mesh['kvh'=8,'seq'=32] {'seq'}, dimensions={0} | all-to-all | bytes 131072 | tf_op jit(solution)/shard_map/all_to_all | solution.py:220
  36.6 0.0 copy-done.3
  36.6 0.9 shard_map.133
  37.5 12.8 %all_to_all.32.got_ref = bf16[8,16,512]{2,1,0:T(8,128)(2,1)S(1)} all-to-all(bf16[8,16,512]{2,1,0:T(8,128)(2,1)S(1)} %get-tuple-element.10), channel_id=1, replica_groups=mesh['kvh'=8,'seq'=32] {'kvh'}, dimensions={0} | all-to-all | bytes 262144 | tf_op jit(solution)/shard_map/all_to_all | solution.py:220
  50.3 0.0 copy-done
  50.3 0.0 copy-done.1
  50.3 0.0 copy-start.2
  50.3 1.1 %shard_map.134 = (bf16[16,512]{1,0:T(8,128)(2,1)S(1)}, bf16[32,32,128]{2,1,0:T(8,128)(2,1)S(1)}) custom-call(bf16[8,16,512]{2,1,0:T(8,128)(2,1)S(1)} %all_to_all.32.got_ref, bf16[16,512]{1,0:T(8,128)(2,1)S(1)} %get-tuple-element.11.residual_ref, f32[1,512]{1,0:T(1,128)S(1)} %get-tuple-element.12.gain_ref, bf16[512,3328]{1,0:T(8,128)(2,1)S(1)} %copy-done, ...), custom_call_target="tpu_custom_call" | custom-call | tf_op jit(solution)/shard_map/pallas_call | solution.py:31
  51.4 12.7 %all_to_all.33.refs_0_ = bf16[32,32,128]{2,1,0:T(8,128)(2,1)S(1)} all-to-all(bf16[32,32,128]{2,1,0:T(8,128)(2,1)S(1)} %get-tuple-element.13), channel_id=1, replica_groups=mesh['kvh'=8,'seq'=32] {'seq'}, dimensions={0} | all-to-all | bytes 524288 | tf_op jit(solution)/shard_map/all_to_all | solution.py:220
  64.1 0.2 shard_map.135
  64.3 15.0 %all_to_all.34.got_ref = bf16[32,16,128]{2,1,0:T(8,128)(2,1)S(1)} all-to-all(bf16[32,16,128]{2,1,0:T(8,128)(2,1)S(1)} %shard_map.135), channel_id=1, replica_groups=mesh['kvh'=8,'seq'=32] {'seq'}, dimensions={0} | all-to-all | bytes 262144 | tf_op jit(solution)/shard_map/all_to_all | solution.py:220
  79.3 0.0 copy-done.2
  79.3 0.6 shard_map.136
  79.9 11.0 %all_to_all.35.got_ref = bf16[8,16,512]{2,1,0:T(8,128)(2,1)S(1)} all-to-all(bf16[8,16,512]{2,1,0:T(8,128)(2,1)S(1)} %shard_map.136), channel_id=1, replica_groups=mesh['kvh'=8,'seq'=32] {'kvh'}, dimensions={0} | all-to-all | bytes 262144 | tf_op jit(solution)/shard_map/all_to_all | solution.py:220
  90.8 0.6 shard_map.137
Async XLA Ops:
  0.6 36.0 %copy-start.3 = (bf16[2048,512]{1,0:T(8,128)(2,1)S(1)}, bf16[2048,512]{1,0:T(8,128)(2,1)}, u32[]{:S(2)}) copy-start(bf16[2048,512]{1,0:T(8,128)(2,1)} %weight_ref.2) | copy-start | bytes 6291460
  0.6 49.6 %copy-start = (bf16[512,3328]{1,0:T(8,128)(2,1)S(1)}, bf16[512,3328]{1,0:T(8,128)(2,1)}, u32[]{:S(2)}) copy-start(bf16[512,3328]{1,0:T(8,128)(2,1)} %gate_ref.1) | copy-start | bytes 10223620
  0.7 49.6 %copy-start.1 = (bf16[512,3328]{1,0:T(8,128)(2,1)S(1)}, bf16[512,3328]{1,0:T(8,128)(2,1)}, u32[]{:S(2)}) copy-start(bf16[512,3328]{1,0:T(8,128)(2,1)} %up_ref.1) | copy-start | bytes 10223620
  50.3 29.0 %copy-start.2 = (bf16[3328,512]{1,0:T(8,128)(2,1)S(1)}, bf16[3328,512]{1,0:T(8,128)(2,1)}, u32[]{:S(2)}) copy-start(bf16[3328,512]{1,0:T(8,128)(2,1)} %weight_ref.3) | copy-start | bytes 10223620

commit v2 on v1

--- a/solution.py
+++ b/solution.py
@@ -10,7 +10,7 @@
 F32 = jnp.float32
 LANES = 128
 MIB = 1 << 20
-KEY_PARTS = 4
+CORES = 2
 VMEM = pl.BlockSpec(memory_space=pltpu.VMEM)
 SMEM = pl.BlockSpec(memory_space=pltpu.SMEM)
 HBM = pl.BlockSpec(memory_space=pltpu.HBM)
@@ -79,16 +79,9 @@
     out_ref, kept_ref, row_ref = refs[:3]
     targets, sems = refs[3:11], refs[11]
     len_ref, q_ref, tk_ref, k_ref, tv_ref, v_ref, res_ref, gn_ref = targets
-    chunk = k_ref.shape[0] // KEY_PARTS
-    chunks = [pl.ds(i * chunk, chunk) for i in range(KEY_PARTS)]
-    copies = start_copies(
-        [*sources[:3], *(sources[3].at[c] for c in chunks), *sources[4:]],
-        [*targets[:3], *(targets[3].at[c] for c in chunks), *targets[4:]],
-        sems,
-    )
-    for copy in copies[:3]:
+    copies = start_copies(sources, targets, sems)
+    for copy in copies[:4]:
         copy.wait()
-    keys, others = copies[3 : 3 + KEY_PARTS], copies[3 + KEY_PARTS :]
     requests, heads, size = q_ref.shape
     slots = k_ref.shape[1]
     scale = size ** (-0.5)
@@ -98,8 +91,6 @@
     slot = first + lane_index((heads, slots))
     scores, valid, fresh = [], [], []
     for b in range(requests):
-        if b % chunk == 0:
-            keys[b // chunk].wait()
         q = q_ref[b]
         scores.append(lax.dot_general(q, k_ref[b], contract, preferred_element_type=F32))
         valid.append(jnp.where(slot < len_ref[b], 1.0, 0.0))
@@ -115,7 +106,7 @@
     rounded = weights.astype(BF)
     own = round_bf(own)
     stats = stat_rows((peak,) + two_parts(total)).astype(BF)
-    for copy in others:
+    for copy in copies[4:]:
         copy.wait()
     for b in range(requests):
         rows = slice(b * heads, (b + 1) * heads)
@@ -147,7 +138,7 @@
     )
     attended_ref[...] = attended
     projected = jnp.dot(attended, weight_ref[...], preferred_element_type=F32)
-    out_ref[...] = jnp.broadcast_to(projected.astype(BF)[None], out_ref.shape)
+    out_ref[...] = projected.astype(BF)
 
 
 def gate_up_kernel(
@@ -195,7 +186,7 @@
 
 def down_kernel(got_ref, weight_ref, out_ref, rows_ref):
     pieces, depth, _ = got_ref.shape
-    requests = out_ref.shape[1]
+    requests = out_ref.shape[0]
     halves = pieces // requests
     blocks = weight_ref.shape[0] // (halves * LANES)
     rows_ref[...] = got_ref[...].astype(F32).reshape(rows_ref.shape)
@@ -208,7 +199,7 @@
         -1,
     )
     down = jnp.dot(hidden, weight_ref[...], preferred_element_type=F32)
-    out_ref[...] = jnp.broadcast_to(down.astype(BF)[None], out_ref.shape)
+    out_ref[...] = down.astype(BF)
 
 
 def finish_kernel(got_ref, middle_ref, out_ref):
@@ -216,8 +207,21 @@
     out_ref[...] = (middle_ref[...].astype(F32) + down).astype(BF)
 
 
+def add_kernel(a_ref, b_ref, out_ref):
+    total = (a_ref[...].astype(F32) + b_ref[...].astype(F32)).astype(BF)
+    out_ref[...] = jnp.broadcast_to(total[None], out_ref.shape)
+
+
 def exchange(pieces, axis):
     return lax.all_to_all(pieces, axis, 0, 0)
+
+
+def parts_kvh(value):
+    size = lax.axis_size("kvh")
+    other = lax.ppermute(value, "kvh", [(i, i ^ 1) for i in range(size)])
+    both = call(add_kernel, bf(size // CORES, *value.shape), 2)(value, other)
+    columns = [list(range(core, size, CORES)) for core in range(CORES)]
+    return lax.all_to_all(both, "kvh", 0, 0, axis_index_groups=columns)
 
 
 def shards(
@@ -235,7 +239,7 @@
     down_weight,
 ):
     requests, heads, size = queries.shape
-    seq, kvh = lax.axis_size("seq"), lax.axis_size("kvh")
+    seq = lax.axis_size("seq")
     rows = requests * heads // seq
     width = residual.shape[1]
     halves = seq // requests
@@ -262,7 +266,7 @@
             pltpu.VMEM(cache, BF),
             pltpu.VMEM((requests, width), BF),
             pltpu.VMEM((width // LANES, LANES), BF),
-            DMA((7 + KEY_PARTS,)),
+            DMA((8,)),
         ],
         smem=(0,),
         hbm=range(1, 12),
@@ -284,7 +288,7 @@
     merged = call(merge_kernel, bf(seq, rows, size), 1)(got)
     attended, projected = call(
         project_kernel,
-        (bf(requests, heads * size), bf(kvh, requests, width)),
+        (bf(requests, heads * size), bf(requests, width)),
         2,
         scratch=[pltpu.VMEM((requests * heads, size), F32)],
     )(exchange(merged, "seq"), out_weight)
@@ -295,17 +299,17 @@
         scratch=[
             pltpu.VMEM((seq * depth, LANES), F32),
         ],
-    )(exchange(projected, "kvh"), residual, gain, gate_weight, up_weight)
+    )(parts_kvh(projected), residual, gain, gate_weight, up_weight)
     hidden = call(lambda *refs: hidden_kernel(blocks, *refs), bf(seq, thin, LANES), 1)(
         exchange(pieces, "seq")
     )
     down = call(
         down_kernel,
-        bf(kvh, requests, width),
+        bf(requests, width),
         2,
         scratch=[pltpu.VMEM((seq * thin, LANES), F32)],
     )(exchange(hidden, "seq"), down_weight)
-    updated = call(finish_kernel, bf(requests, width), 2)(exchange(down, "kvh"), middle)
+    updated = call(finish_kernel, bf(requests, width), 2)(parts_kvh(down), middle)
     return (updated, attended)
 
 

time: 91.7 us -> 91.5 us (level)
  blocking collectives: 84.7 us -> 75.7 us
  starting transfers between devices: 0 us -> 7.32 us
  waiting for transfers between devices: 0 us -> 1.68 us
    all_to_all x6 -> x4, blocking collectives: 84.7 us -> 60.4 us  [exchange(): return lax.all_to_all(pieces, axis, 0, 0)]
    all_to_all x0 -> x2, blocking collectives: none -> 15.3 us  [parts_kvh(): return lax.all_to_all(both, 'kvh', 0, 0, axis_index_groups=columns)]
    ppermute x0 -> x2, starting transfers between devices: none -> 7.32 us  [parts_kvh(): other = lax.ppermute(value, 'kvh', [(i, i ^ 1) for i in range(size)])]
    ppermute x0 -> x2, waiting for transfers between devices: none -> 1.68 us  [parts_kvh(): other = lax.ppermute(value, 'kvh', [(i, i ^ 1) for i in range(size)])]
    pallas_call x7 -> x9, Pallas kernels: 5.98 us -> 5.76 us  [run(): kernel(*[pltpu.with_memory_space_constraint(arg, pltpu.HBM) if i in hbm e...]
  transfers between devices with their start and end apart: 0 -> 2, of which waited for: 0 -> 2; matrix products, arithmetic and copies ran while one was open for 0% -> 0% of each run, Pallas kernels for 0% -> 0%
where the time goes in v2:
time: 91.5 us; the launch traced here: 91.2 us
  blocking collectives  75.7 us (83%)
  starting transfers between devices  7.32 us (8%)
  Pallas kernels  5.76 us (6%)
  waiting for transfers between devices  1.68 us (2%)
    all_to_all x4, blocking collectives, exchange(): return lax.all_to_all(pieces, axis, 0, 0)  60.4 us
    all_to_all x2, blocking collectives, parts_kvh(): return lax.all_to_all(both, 'kvh', 0, 0, axis_index_groups=columns)  15.3 us
    ppermute x2, starting transfers between devices, parts_kvh(): other = lax.ppermute(value, 'kvh', [(i, i ^ 1) for i in range(size)])  7.32 us
    pallas_call x9, Pallas kernels, run(): kernel(*[pltpu.with_memory_space_constraint(arg, pltpu.HBM) if i in hbm e...  5.76 us
  transfers between devices with their start and end apart: 2, of which 2 were waited for; matrix products, arithmetic and copies ran while one was open for 0% of the time, Pallas kernels for 0%

profile of v2, /device:TPU:1, one launch (start us, length us, event | category | flops | bytes accessed | tf_op | source)
XLA Modules:
  0.0 91.2 jit_solution(16222191949550399580)
XLA Ops:
  0.6 0.0 copy-start.3
  0.6 0.0 copy-start
  0.7 0.0 copy-start.1
  0.7 2.1 %shard_map.131 = (bf16[16,16,256]{2,1,0:T(8,128)(2,1)S(1)}, bf16[16,512]{1,0:T(8,128)(2,1)S(1)}, f32[1,512]{1,0:T(1,128)S(1)}) custom-call(s32[1]{0:T(128)} %bitcast.where_ref, s32[16]{0:T(128)} %refs_0_.1, bf16[16,16,128]{2,1,0:T(8,128)(2,1)} %refs_1_.1, bf16[16,128]{1,0:T(8,128)(2,1)} %bitcast.10, bf16[16,128,128]{2,1,0:T(8,128)(2,1)} %bitcast.8, ...), custom_call_target="tpu_custom_call" | custom-call | tf_op jit(solution)/shard_map/pallas_call | solution.py:31
  2.8 21.1 %all_to_all.30.got_ref = bf16[32,8,256]{2,1,0:T(8,128)(2,1)S(1)} all-to-all(bf16[32,8,256]{2,1,0:T(8,128)(2,1)S(1)} %bitcast.7), channel_id=1, replica_groups=mesh['kvh'=8,'seq'=32] {'seq'}, dimensions={0} | all-to-all | bytes 262144 | tf_op jit(solution)/shard_map/all_to_all | solution.py:216
  23.9 0.2 shard_map.132
  24.1 12.4 %all_to_all.31.got_ref = bf16[32,8,128]{2,1,0:T(8,128)(2,1)S(1)} all-to-all(bf16[32,8,128]{2,1,0:T(8,128)(2,1)S(1)} %shard_map.132), channel_id=1, replica_groups=mesh['kvh'=8,'seq'=32] {'seq'}, dimensions={0} | all-to-all | bytes 131072 | tf_op jit(solution)/shard_map/all_to_all | solution.py:216
  36.5 0.0 copy-done.3
  36.5 0.9 shard_map.133
  37.4 3.3 %collective-permute-start = (bf16[16,512]{1,0:T(8,128)(2,1)S(1)}, bf16[16,512]{1,0:T(8,128)(2,1)S(1)}, u32[]{:S(2)}, u32[]{:S(2)}) collective-permute-start(bf16[16,512]{1,0:T(8,128)(2,1)S(1)} %get-tuple-element.10.a_ref), channel_id=1, source_target_pairs={{0,32},{32,0},{64,96},{96,64},{128,160},{160,128},{192,224},{224,1... | collective-permute-start | bytes 49160 | tf_op jit(solution)/shard_map/ppermute | solution.py:221
  40.6 0.8 collective-permute-done.b_ref
  41.5 8.5 %all_to_all.32.got_ref = bf16[4,16,512]{2,1,0:T(8,128)(2,1)S(1)} all-to-all(bf16[4,16,512]{2,1,0:T(8,128)(2,1)S(1)} %shard_map.134), channel_id=1, replica_groups={{0,64,128,192},{32,96,160,224},{1,65,129,193},{33,97,161,225},{2,66,130..., dimensions={0} | all-to-all | bytes 131072 | tf_op jit(solution)/shard_map/all_to_all | solution.py:224
  50.0 0.0 copy-done
  50.0 0.0 copy-done.1
  50.0 0.0 copy-start.2
  50.0 1.2 %shard_map.135 = (bf16[16,512]{1,0:T(8,128)(2,1)S(1)}, bf16[32,32,128]{2,1,0:T(8,128)(2,1)S(1)}) custom-call(bf16[4,16,512]{2,1,0:T(8,128)(2,1)S(1)} %all_to_all.32.got_ref, bf16[16,512]{1,0:T(8,128)(2,1)S(1)} %get-tuple-element.11.residual_ref, f32[1,512]{1,0:T(1,128)S(1)} %get-tuple-element.12.gain_ref, bf16[512,3328]{1,0:T(8,128)(2,1)S(1)} %copy-done, ...), custom_call_target="tpu_custom_call" | custom-call | tf_op jit(solution)/shard_map/pallas_call | solution.py:31
  51.1 12.6 %all_to_all.33.refs_0_ = bf16[32,32,128]{2,1,0:T(8,128)(2,1)S(1)} all-to-all(bf16[32,32,128]{2,1,0:T(8,128)(2,1)S(1)} %get-tuple-element.13), channel_id=1, replica_groups=mesh['kvh'=8,'seq'=32] {'seq'}, dimensions={0} | all-to-all | bytes 524288 | tf_op jit(solution)/shard_map/all_to_all | solution.py:216
  63.8 0.2 shard_map.136
  63.9 14.3 %all_to_all.34.got_ref = bf16[32,16,128]{2,1,0:T(8,128)(2,1)S(1)} all-to-all(bf16[32,16,128]{2,1,0:T(8,128)(2,1)S(1)} %shard_map.136), channel_id=1, replica_groups=mesh['kvh'=8,'seq'=32] {'seq'}, dimensions={0} | all-to-all | bytes 262144 | tf_op jit(solution)/shard_map/all_to_all | solution.py:216
  78.2 0.0 copy-done.2
  78.2 0.6 shard_map.137.a_ref
  78.8 4.0 %collective-permute-start.1 = (bf16[16,512]{1,0:T(8,128)(2,1)S(1)}, bf16[16,512]{1,0:T(8,128)(2,1)S(1)}, u32[]{:S(2)}, u32[]{:S(2)}) collective-permute-start(bf16[16,512]{1,0:T(8,128)(2,1)S(1)} %shard_map.137.a_ref), channel_id=1, source_target_pairs={{0,32},{32,0},{64,96},{96,64},{128,160},{160,128},{192,224},{224,1... | collective-permute-start | bytes 49160 | tf_op jit(solution)/shard_map/ppermute | solution.py:221
  82.9 0.8 collective-permute-done.1.b_ref
  83.7 6.8 %all_to_all.35.got_ref = bf16[4,16,512]{2,1,0:T(8,128)(2,1)S(1)} all-to-all(bf16[4,16,512]{2,1,0:T(8,128)(2,1)S(1)} %shard_map.138), channel_id=1, replica_groups={{0,64,128,192},{32,96,160,224},{1,65,129,193},{33,97,161,225},{2,66,130..., dimensions={0} | all-to-all | bytes 131072 | tf_op jit(solution)/shard_map/all_to_all | solution.py:224
  90.5 0.6 shard_map.139
  (2 shorter events, 0.0 us)
Async XLA Ops:
  0.6 35.9 %copy-start.3 = (bf16[2048,512]{1,0:T(8,128)(2,1)S(1)}, bf16[2048,512]{1,0:T(8,128)(2,1)}, u32[]{:S(2)}) copy-start(bf16[2048,512]{1,0:T(8,128)(2,1)} %weight_ref.2) | copy-start | bytes 6291460
  0.6 49.3 %copy-start = (bf16[512,3328]{1,0:T(8,128)(2,1)S(1)}, bf16[512,3328]{1,0:T(8,128)(2,1)}, u32[]{:S(2)}) copy-start(bf16[512,3328]{1,0:T(8,128)(2,1)} %gate_ref.1) | copy-start | bytes 10223620
  0.7 49.3 %copy-start.1 = (bf16[512,3328]{1,0:T(8,128)(2,1)S(1)}, bf16[512,3328]{1,0:T(8,128)(2,1)}, u32[]{:S(2)}) copy-start(bf16[512,3328]{1,0:T(8,128)(2,1)} %up_ref.1) | copy-start | bytes 10223620
  37.4 4.1 %collective-permute-start = (bf16[16,512]{1,0:T(8,128)(2,1)S(1)}, bf16[16,512]{1,0:T(8,128)(2,1)S(1)}, u32[]{:S(2)}, u32[]{:S(2)}) collective-permute-start(bf16[16,512]{1,0:T(8,128)(2,1)S(1)} %get-tuple-element.10.a_ref), channel_id=1, source_target_pairs={{0,32},{32,0},{64,96},{96,64},{128,160},{160,128},{192,224},{224,1... | collective-permute-start | bytes 49160 | tf_op jit(solution)/shard_map/ppermute | solution.py:221
  50.0 28.3 %copy-start.2 = (bf16[3328,512]{1,0:T(8,128)(2,1)S(1)}, bf16[3328,512]{1,0:T(8,128)(2,1)}, u32[]{:S(2)}) copy-start(bf16[3328,512]{1,0:T(8,128)(2,1)} %weight_ref.3) | copy-start | bytes 10223620
  78.8 4.9 %collective-permute-start.1 = (bf16[16,512]{1,0:T(8,128)(2,1)S(1)}, bf16[16,512]{1,0:T(8,128)(2,1)S(1)}, u32[]{:S(2)}, u32[]{:S(2)}) collective-permute-start(bf16[16,512]{1,0:T(8,128)(2,1)S(1)} %shard_map.137.a_ref), channel_id=1, source_target_pairs={{0,32},{32,0},{64,96},{96,64},{128,160},{160,128},{192,224},{224,1... | collective-permute-start | bytes 49160 | tf_op jit(solution)/shard_map/ppermute | solution.py:221

commit v3 on v1

--- a/solution.py
+++ b/solution.py
@@ -10,7 +10,7 @@
 F32 = jnp.float32
 LANES = 128
 MIB = 1 << 20
-KEY_PARTS = 4
+FAST = {"seq": 8, "kvh": 2}
 VMEM = pl.BlockSpec(memory_space=pltpu.VMEM)
 SMEM = pl.BlockSpec(memory_space=pltpu.SMEM)
 HBM = pl.BlockSpec(memory_space=pltpu.HBM)
@@ -79,16 +79,9 @@
     out_ref, kept_ref, row_ref = refs[:3]
     targets, sems = refs[3:11], refs[11]
     len_ref, q_ref, tk_ref, k_ref, tv_ref, v_ref, res_ref, gn_ref = targets
-    chunk = k_ref.shape[0] // KEY_PARTS
-    chunks = [pl.ds(i * chunk, chunk) for i in range(KEY_PARTS)]
-    copies = start_copies(
-        [*sources[:3], *(sources[3].at[c] for c in chunks), *sources[4:]],
-        [*targets[:3], *(targets[3].at[c] for c in chunks), *targets[4:]],
-        sems,
-    )
-    for copy in copies[:3]:
+    copies = start_copies(sources, targets, sems)
+    for copy in copies[:4]:
         copy.wait()
-    keys, others = copies[3 : 3 + KEY_PARTS], copies[3 + KEY_PARTS :]
     requests, heads, size = q_ref.shape
     slots = k_ref.shape[1]
     scale = size ** (-0.5)
@@ -98,8 +91,6 @@
     slot = first + lane_index((heads, slots))
     scores, valid, fresh = [], [], []
     for b in range(requests):
-        if b % chunk == 0:
-            keys[b // chunk].wait()
         q = q_ref[b]
         scores.append(lax.dot_general(q, k_ref[b], contract, preferred_element_type=F32))
         valid.append(jnp.where(slot < len_ref[b], 1.0, 0.0))
@@ -115,7 +106,7 @@
     rounded = weights.astype(BF)
     own = round_bf(own)
     stats = stat_rows((peak,) + two_parts(total)).astype(BF)
-    for copy in others:
+    for copy in copies[4:]:
         copy.wait()
     for b in range(requests):
         rows = slice(b * heads, (b + 1) * heads)
@@ -217,7 +208,9 @@
 
 
 def exchange(pieces, axis):
-    return lax.all_to_all(pieces, axis, 0, 0)
+    size, fast = lax.axis_size(axis), FAST[axis]
+    order = [slow * fast + last for last in range(fast) for slow in range(size // fast)]
+    return lax.all_to_all(pieces, axis, 0, 0, axis_index_groups=[order])
 
 
 def shards(
@@ -262,7 +255,7 @@
             pltpu.VMEM(cache, BF),
             pltpu.VMEM((requests, width), BF),
             pltpu.VMEM((width // LANES, LANES), BF),
-            DMA((7 + KEY_PARTS,)),
+            DMA((8,)),
         ],
         smem=(0,),
         hbm=range(1, 12),

time: 91.7 us -> 91.4 us (level)
  no operation moved by 1% of the time
where the time goes in v3:
time: 91.4 us; the launch traced here: 91.1 us
  blocking collectives  84.6 us (93%)
  Pallas kernels  5.75 us (6%)
    all_to_all x6, blocking collectives, exchange(): return lax.all_to_all(pieces, axis, 0, 0, axis_index_groups=[order])  84.6 us
    pallas_call x7, Pallas kernels, run(): kernel(*[pltpu.with_memory_space_constraint(arg, pltpu.HBM) if i in hbm e...  5.75 us

profile of v3, /device:TPU:1, one launch (start us, length us, event | category | flops | bytes accessed | tf_op | source)
XLA Modules:
  0.0 91.1 jit_solution(7180322267380519)
XLA Ops:
  0.6 0.0 copy-start.3
  0.6 0.0 copy-start
  0.7 0.0 copy-start.1
  0.7 2.1 %shard_map.131 = (bf16[16,16,256]{2,1,0:T(8,128)(2,1)S(1)}, bf16[16,512]{1,0:T(8,128)(2,1)S(1)}, f32[1,512]{1,0:T(1,128)S(1)}) custom-call(s32[1]{0:T(128)} %bitcast.where_ref, s32[16]{0:T(128)} %refs_0_.1, bf16[16,16,128]{2,1,0:T(8,128)(2,1)} %refs_1_.1, bf16[16,128]{1,0:T(8,128)(2,1)} %bitcast.10, bf16[16,128,128]{2,1,0:T(8,128)(2,1)} %bitcast.8, ...), custom_call_target="tpu_custom_call" | custom-call | tf_op jit(solution)/shard_map/pallas_call | solution.py:31
  2.8 21.3 %all_to_all.30.got_ref = bf16[32,8,256]{2,1,0:T(8,128)(2,1)S(1)} all-to-all(bf16[32,8,256]{2,1,0:T(8,128)(2,1)S(1)} %bitcast.7), channel_id=1, replica_groups={{0,8,16,24,1,9,17,25,2,10,18,26,3,11,19,27,4,12,20,28,5,13,21,29,6,14,2..., dimensions={0} | all-to-all | bytes 262144 | tf_op jit(solution)/shard_map/all_to_all | solution.py:213
  24.1 0.2 shard_map.132
  24.3 12.1 %all_to_all.31.got_ref = bf16[32,8,128]{2,1,0:T(8,128)(2,1)S(1)} all-to-all(bf16[32,8,128]{2,1,0:T(8,128)(2,1)S(1)} %shard_map.132), channel_id=1, replica_groups={{0,8,16,24,1,9,17,25,2,10,18,26,3,11,19,27,4,12,20,28,5,13,21,29,6,14,2..., dimensions={0} | all-to-all | bytes 131072 | tf_op jit(solution)/shard_map/all_to_all | solution.py:213
  36.4 0.0 copy-done.3
  36.4 0.9 shard_map.133
  37.3 12.6 %all_to_all.32.got_ref = bf16[8,16,512]{2,1,0:T(8,128)(2,1)S(1)} all-to-all(bf16[8,16,512]{2,1,0:T(8,128)(2,1)S(1)} %get-tuple-element.10), channel_id=1, replica_groups={{0,64,128,192,32,96,160,224},{1,65,129,193,33,97,161,225},{2,66,130,194..., dimensions={0} | all-to-all | bytes 262144 | tf_op jit(solution)/shard_map/all_to_all | solution.py:213
  49.9 0.0 copy-done
  50.0 0.0 copy-done.1
  50.0 0.0 copy-start.2
  50.0 1.1 %shard_map.134 = (bf16[16,512]{1,0:T(8,128)(2,1)S(1)}, bf16[32,32,128]{2,1,0:T(8,128)(2,1)S(1)}) custom-call(bf16[8,16,512]{2,1,0:T(8,128)(2,1)S(1)} %all_to_all.32.got_ref, bf16[16,512]{1,0:T(8,128)(2,1)S(1)} %get-tuple-element.11.residual_ref, f32[1,512]{1,0:T(1,128)S(1)} %get-tuple-element.12.gain_ref, bf16[512,3328]{1,0:T(8,128)(2,1)S(1)} %copy-done, ...), custom_call_target="tpu_custom_call" | custom-call | tf_op jit(solution)/shard_map/pallas_call | solution.py:31
  51.1 14.5 %all_to_all.33.refs_0_ = bf16[32,32,128]{2,1,0:T(8,128)(2,1)S(1)} all-to-all(bf16[32,32,128]{2,1,0:T(8,128)(2,1)S(1)} %get-tuple-element.13), channel_id=1, replica_groups={{0,8,16,24,1,9,17,25,2,10,18,26,3,11,19,27,4,12,20,28,5,13,21,29,6,14,2..., dimensions={0} | all-to-all | bytes 524288 | tf_op jit(solution)/shard_map/all_to_all | solution.py:213
  65.6 0.2 shard_map.135
  65.8 13.7 %all_to_all.34.got_ref = bf16[32,16,128]{2,1,0:T(8,128)(2,1)S(1)} all-to-all(bf16[32,16,128]{2,1,0:T(8,128)(2,1)S(1)} %shard_map.135), channel_id=1, replica_groups={{0,8,16,24,1,9,17,25,2,10,18,26,3,11,19,27,4,12,20,28,5,13,21,29,6,14,2..., dimensions={0} | all-to-all | bytes 262144 | tf_op jit(solution)/shard_map/all_to_all | solution.py:213
  79.5 0.0 copy-done.2
  79.5 0.6 shard_map.136
  80.1 10.4 %all_to_all.35.got_ref = bf16[8,16,512]{2,1,0:T(8,128)(2,1)S(1)} all-to-all(bf16[8,16,512]{2,1,0:T(8,128)(2,1)S(1)} %shard_map.136), channel_id=1, replica_groups={{0,64,128,192,32,96,160,224},{1,65,129,193,33,97,161,225},{2,66,130,194..., dimensions={0} | all-to-all | bytes 262144 | tf_op jit(solution)/shard_map/all_to_all | solution.py:213
  90.5 0.6 shard_map.137
Async XLA Ops:
  0.6 35.8 %copy-start.3 = (bf16[2048,512]{1,0:T(8,128)(2,1)S(1)}, bf16[2048,512]{1,0:T(8,128)(2,1)}, u32[]{:S(2)}) copy-start(bf16[2048,512]{1,0:T(8,128)(2,1)} %weight_ref.2) | copy-start | bytes 6291460
  0.6 49.3 %copy-start = (bf16[512,3328]{1,0:T(8,128)(2,1)S(1)}, bf16[512,3328]{1,0:T(8,128)(2,1)}, u32[]{:S(2)}) copy-start(bf16[512,3328]{1,0:T(8,128)(2,1)} %gate_ref.1) | copy-start | bytes 10223620
  0.7 49.3 %copy-start.1 = (bf16[512,3328]{1,0:T(8,128)(2,1)S(1)}, bf16[512,3328]{1,0:T(8,128)(2,1)}, u32[]{:S(2)}) copy-start(bf16[512,3328]{1,0:T(8,128)(2,1)} %up_ref.1) | copy-start | bytes 10223620
  50.0 29.5 %copy-start.2 = (bf16[3328,512]{1,0:T(8,128)(2,1)S(1)}, bf16[3328,512]{1,0:T(8,128)(2,1)}, u32[]{:S(2)}) copy-start(bf16[3328,512]{1,0:T(8,128)(2,1)} %weight_ref.3) | copy-start | bytes 10223620

commit v4 on v3

--- a/solution.py
+++ b/solution.py
@@ -10,19 +10,21 @@
 F32 = jnp.float32
 LANES = 128
 MIB = 1 << 20
-FAST = {"seq": 8, "kvh": 2}
+CORES = 2
 VMEM = pl.BlockSpec(memory_space=pltpu.VMEM)
 SMEM = pl.BlockSpec(memory_space=pltpu.SMEM)
 HBM = pl.BlockSpec(memory_space=pltpu.HBM)
 DMA = pltpu.SemaphoreType.DMA
 
 
-def call(body, out_shape, n_in, scratch=(), smem=(), hbm=(), limit=16 * MIB):
+def call(body, out_shape, n_in, scratch=(), smem=(), hbm=(), hbm_out=(), limit=16 * MIB):
     kernel = pl.pallas_call(
         body,
         out_shape=out_shape,
         in_specs=[SMEM if i in smem else HBM if i in hbm else VMEM for i in range(n_in)],
-        out_specs=jax.tree.map(lambda _: VMEM, out_shape),
+        out_specs=tuple(HBM if i in hbm_out else VMEM for i in range(len(out_shape)))
+        if isinstance(out_shape, tuple)
+        else VMEM,
         scratch_shapes=list(scratch),
         compiler_params=pltpu.CompilerParams(vmem_limit_bytes=limit),
     )
@@ -142,8 +144,10 @@
 
 
 def gate_up_kernel(
-    got_ref, residual_ref, gain_ref, gate_ref, up_ref, middle_ref, out_ref, rows_ref
+    got_ref, residual_ref, gain_ref, gate_ref, up_ref, attended_ref,
+    middle_ref, out_ref, result_ref, rows_ref, sems,
 ):
+    writes = start_copies([attended_ref], [result_ref], sems)
     pieces, depth, _ = out_ref.shape
     requests = residual_ref.shape[0]
     halves = pieces // requests
@@ -169,6 +173,8 @@
         for row in range(2 * blocks + 1, depth):
             put(row, half, zeros)
     out_ref[...] = rows_ref[...].astype(BF).reshape(out_ref.shape)
+    for write in writes:
+        write.wait()
 
 
 def hidden_kernel(blocks, got_ref, out_ref):
@@ -208,9 +214,13 @@
 
 
 def exchange(pieces, axis):
-    size, fast = lax.axis_size(axis), FAST[axis]
-    order = [slow * fast + last for last in range(fast) for slow in range(size // fast)]
-    return lax.all_to_all(pieces, axis, 0, 0, axis_index_groups=[order])
+    return lax.all_to_all(pieces, axis, 0, 0)
+
+
+def parts_kvh(pieces):
+    size = lax.axis_size("kvh")
+    order = [chip * CORES + core for core in range(CORES) for chip in range(size // CORES)]
+    return lax.all_to_all(pieces, "kvh", 0, 0, axis_index_groups=[order])
 
 
 def shards(
@@ -281,14 +291,13 @@
         2,
         scratch=[pltpu.VMEM((requests * heads, size), F32)],
     )(exchange(merged, "seq"), out_weight)
-    middle, pieces = call(
+    middle, pieces, attended = call(
         gate_up_kernel,
-        (bf(requests, width), bf(seq, depth, LANES)),
-        5,
-        scratch=[
-            pltpu.VMEM((seq * depth, LANES), F32),
-        ],
-    )(exchange(projected, "kvh"), residual, gain, gate_weight, up_weight)
+        (bf(requests, width), bf(seq, depth, LANES), bf(requests, heads * size)),
+        6,
+        scratch=[pltpu.VMEM((seq * depth, LANES), F32), DMA((1,))],
+        hbm_out=(2,),
+    )(parts_kvh(projected), residual, gain, gate_weight, up_weight, attended)
     hidden = call(lambda *refs: hidden_kernel(blocks, *refs), bf(seq, thin, LANES), 1)(
         exchange(pieces, "seq")
     )
@@ -298,7 +307,7 @@
         2,
         scratch=[pltpu.VMEM((seq * thin, LANES), F32)],
     )(exchange(hidden, "seq"), down_weight)
-    updated = call(finish_kernel, bf(requests, width), 2)(exchange(down, "kvh"), middle)
+    updated = call(finish_kernel, bf(requests, width), 2)(parts_kvh(down), middle)
     return (updated, attended)
 
 

time: 91.4 us -> 90.9 us (level)
  no operation moved by 1% of the time
where the time goes in v4:
time: 90.9 us; the launch traced here: 90.6 us
  blocking collectives  84.6 us (93%)
  Pallas kernels  5.28 us (6%)
    all_to_all x4, blocking collectives, exchange(): return lax.all_to_all(pieces, axis, 0, 0)  62 us
    all_to_all x2, blocking collectives, parts_kvh(): return lax.all_to_all(pieces, 'kvh', 0, 0, axis_index_groups=[order])  22.6 us
    pallas_call x7, Pallas kernels, run(): kernel(*[pltpu.with_memory_space_constraint(arg, pltpu.HBM) if i in hbm e...  5.28 us

profile of v4, /device:TPU:1, one launch (start us, length us, event | category | flops | bytes accessed | tf_op | source)
XLA Modules:
  0.0 90.6 jit_solution(13508091496072556617)
XLA Ops:
  0.6 0.0 copy-start.3
  0.6 0.0 copy-start.1
  0.7 0.0 copy-start.2
  0.7 2.1 %shard_map.131 = (bf16[16,16,256]{2,1,0:T(8,128)(2,1)S(1)}, bf16[16,512]{1,0:T(8,128)(2,1)S(1)}, f32[1,512]{1,0:T(1,128)S(1)}) custom-call(s32[1]{0:T(128)} %bitcast.where_ref, s32[16]{0:T(128)} %refs_0_.1, bf16[16,16,128]{2,1,0:T(8,128)(2,1)} %refs_1_.1, bf16[16,128]{1,0:T(8,128)(2,1)} %bitcast.10, bf16[16,128,128]{2,1,0:T(8,128)(2,1)} %bitcast.8, ...), custom_call_target="tpu_custom_call" | custom-call | tf_op jit(solution)/shard_map/pallas_call | solution.py:33
  2.8 21.1 %all_to_all.30.got_ref = bf16[32,8,256]{2,1,0:T(8,128)(2,1)S(1)} all-to-all(bf16[32,8,256]{2,1,0:T(8,128)(2,1)S(1)} %bitcast.7), channel_id=1, replica_groups=mesh['kvh'=8,'seq'=32] {'seq'}, dimensions={0} | all-to-all | bytes 262144 | tf_op jit(solution)/shard_map/all_to_all | solution.py:217
  23.9 0.2 shard_map.132
  24.1 12.4 %all_to_all.31.got_ref = bf16[32,8,128]{2,1,0:T(8,128)(2,1)S(1)} all-to-all(bf16[32,8,128]{2,1,0:T(8,128)(2,1)S(1)} %shard_map.132), channel_id=1, replica_groups=mesh['kvh'=8,'seq'=32] {'seq'}, dimensions={0} | all-to-all | bytes 131072 | tf_op jit(solution)/shard_map/all_to_all | solution.py:217
  36.5 0.0 copy-done.3
  36.5 0.4 shard_map.133
  36.9 12.7 %all_to_all.32.got_ref = bf16[8,16,512]{2,1,0:T(8,128)(2,1)S(1)} all-to-all(bf16[8,16,512]{2,1,0:T(8,128)(2,1)S(1)} %get-tuple-element.11), channel_id=1, replica_groups={{0,64,128,192,32,96,160,224},{1,65,129,193,33,97,161,225},{2,66,130,194..., dimensions={0} | all-to-all | bytes 262144 | tf_op jit(solution)/shard_map/all_to_all | solution.py:223
  49.6 0.0 copy-done.1
  49.6 0.0 copy-done.2
  49.6 0.0 copy-start
  49.6 1.2 %shard_map.134 = (bf16[16,512]{1,0:T(8,128)(2,1)S(1)}, bf16[32,32,128]{2,1,0:T(8,128)(2,1)S(1)}, bf16[16,2048]{1,0:T(8,128)(2,1)}) custom-call(bf16[8,16,512]{2,1,0:T(8,128)(2,1)S(1)} %all_to_all.32.got_ref, bf16[16,512]{1,0:T(8,128)(2,1)S(1)} %get-tuple-element.12.residual_ref, f32[1,512]{1,0:T(1,128)S(1)} %get-tuple-element.13.gain_ref, ...), custom_call_target="tpu_custom_call" | custom-call | tf_op jit(solution)/shard_map/pallas_call | solution.py:33
  50.8 12.9 %all_to_all.33.refs_0_ = bf16[32,32,128]{2,1,0:T(8,128)(2,1)S(1)} all-to-all(bf16[32,32,128]{2,1,0:T(8,128)(2,1)S(1)} %get-tuple-element.15), channel_id=1, replica_groups=mesh['kvh'=8,'seq'=32] {'seq'}, dimensions={0} | all-to-all | bytes 524288 | tf_op jit(solution)/shard_map/all_to_all | solution.py:217
  63.7 0.2 shard_map.135
  63.9 15.6 %all_to_all.34.got_ref = bf16[32,16,128]{2,1,0:T(8,128)(2,1)S(1)} all-to-all(bf16[32,16,128]{2,1,0:T(8,128)(2,1)S(1)} %shard_map.135), channel_id=1, replica_groups=mesh['kvh'=8,'seq'=32] {'seq'}, dimensions={0} | all-to-all | bytes 262144 | tf_op jit(solution)/shard_map/all_to_all | solution.py:217
  79.5 0.0 copy-done
  79.5 0.6 shard_map.136
  80.1 9.9 %all_to_all.35.got_ref = bf16[8,16,512]{2,1,0:T(8,128)(2,1)S(1)} all-to-all(bf16[8,16,512]{2,1,0:T(8,128)(2,1)S(1)} %shard_map.136), channel_id=1, replica_groups={{0,64,128,192,32,96,160,224},{1,65,129,193,33,97,161,225},{2,66,130,194..., dimensions={0} | all-to-all | bytes 262144 | tf_op jit(solution)/shard_map/all_to_all | solution.py:223
  90.0 0.6 shard_map.137
Async XLA Ops:
  0.6 35.9 %copy-start.3 = (bf16[2048,512]{1,0:T(8,128)(2,1)S(1)}, bf16[2048,512]{1,0:T(8,128)(2,1)}, u32[]{:S(2)}) copy-start(bf16[2048,512]{1,0:T(8,128)(2,1)} %weight_ref.2) | copy-start | bytes 6291460
  0.6 49.0 %copy-start.1 = (bf16[512,3328]{1,0:T(8,128)(2,1)S(1)}, bf16[512,3328]{1,0:T(8,128)(2,1)}, u32[]{:S(2)}) copy-start(bf16[512,3328]{1,0:T(8,128)(2,1)} %gate_ref.1) | copy-start | bytes 10223620
  0.7 48.9 %copy-start.2 = (bf16[512,3328]{1,0:T(8,128)(2,1)S(1)}, bf16[512,3328]{1,0:T(8,128)(2,1)}, u32[]{:S(2)}) copy-start(bf16[512,3328]{1,0:T(8,128)(2,1)} %up_ref.1) | copy-start | bytes 10223620
  49.6 29.9 %copy-start = (bf16[3328,512]{1,0:T(8,128)(2,1)S(1)}, bf16[3328,512]{1,0:T(8,128)(2,1)}, u32[]{:S(2)}) copy-start(bf16[3328,512]{1,0:T(8,128)(2,1)} %weight_ref.3) | copy-start | bytes 10223620

commit v5 on v2

--- a/solution.py
+++ b/solution.py
@@ -17,12 +17,14 @@
 DMA = pltpu.SemaphoreType.DMA
 
 
-def call(body, out_shape, n_in, scratch=(), smem=(), hbm=(), limit=16 * MIB):
+def call(body, out_shape, n_in, scratch=(), smem=(), hbm=(), hbm_out=(), limit=16 * MIB):
     kernel = pl.pallas_call(
         body,
         out_shape=out_shape,
         in_specs=[SMEM if i in smem else HBM if i in hbm else VMEM for i in range(n_in)],
-        out_specs=jax.tree.map(lambda _: VMEM, out_shape),
+        out_specs=tuple(HBM if i in hbm_out else VMEM for i in range(len(out_shape)))
+        if isinstance(out_shape, tuple)
+        else VMEM,
         scratch_shapes=list(scratch),
         compiler_params=pltpu.CompilerParams(vmem_limit_bytes=limit),
     )
@@ -79,10 +81,16 @@
     out_ref, kept_ref, row_ref = refs[:3]
     targets, sems = refs[3:11], refs[11]
     len_ref, q_ref, tk_ref, k_ref, tv_ref, v_ref, res_ref, gn_ref = targets
-    copies = start_copies(sources, targets, sems)
-    for copy in copies[:4]:
+    requests, heads, size = q_ref.shape
+    halves = [pl.ds(i * requests // 2, requests // 2) for i in range(2)]
+    large = [i for i in range(len(targets)) if targets[i] is k_ref or targets[i] is v_ref]
+    small = [i for i in range(len(targets)) if i not in large]
+    pairs = [(sources[i].at[h], targets[i].at[h]) for i in large for h in halves]
+    pairs += [(sources[i], targets[i]) for i in small]
+    copies = start_copies(*zip(*pairs), sems)
+    keys, values, others = copies[:2], copies[2:4], copies[4:]
+    for copy in keys + others:
         copy.wait()
-    requests, heads, size = q_ref.shape
     slots = k_ref.shape[1]
     scale = size ** (-0.5)
     first = where_ref[0] * slots
@@ -106,7 +114,7 @@
     rounded = weights.astype(BF)
     own = round_bf(own)
     stats = stat_rows((peak,) + two_parts(total)).astype(BF)
-    for copy in copies[4:]:
+    for copy in values:
         copy.wait()
     for b in range(requests):
         rows = slice(b * heads, (b + 1) * heads)
@@ -142,12 +150,14 @@
 
 
 def gate_up_kernel(
-    got_ref, residual_ref, gain_ref, gate_ref, up_ref, middle_ref, out_ref, rows_ref
+    where_ref, p0_ref, p1_ref, p2_ref, p3_ref, residual_ref, gain_ref, gate_ref, up_ref,
+    attended_ref, middle_ref, out_ref, result_ref, rows_ref, slots_ref, sems,
 ):
+    writes = start_copies([attended_ref], [result_ref], sems)
     pieces, depth, _ = out_ref.shape
     requests = residual_ref.shape[0]
     halves = pieces // requests
-    projected = jnp.sum(got_ref[...].astype(F32), 0)
+    projected = sum_in_order(where_ref, (p0_ref, p1_ref, p2_ref, p3_ref), slots_ref)
     middle = (residual_ref[...].astype(F32) + projected).astype(BF)
     middle_ref[...] = middle
     middle = middle.astype(F32)
@@ -169,6 +179,8 @@
         for row in range(2 * blocks + 1, depth):
             put(row, half, zeros)
     out_ref[...] = rows_ref[...].astype(BF).reshape(out_ref.shape)
+    for write in writes:
+        write.wait()
 
 
 def hidden_kernel(blocks, got_ref, out_ref):
@@ -202,26 +214,34 @@
     out_ref[...] = down.astype(BF)
 
 
-def finish_kernel(got_ref, middle_ref, out_ref):
-    down = jnp.sum(got_ref[...].astype(F32), 0)
+def finish_kernel(where_ref, p0_ref, p1_ref, p2_ref, p3_ref, middle_ref, out_ref, slots_ref):
+    down = sum_in_order(where_ref, (p0_ref, p1_ref, p2_ref, p3_ref), slots_ref)
     out_ref[...] = (middle_ref[...].astype(F32) + down).astype(BF)
 
 
 def add_kernel(a_ref, b_ref, out_ref):
-    total = (a_ref[...].astype(F32) + b_ref[...].astype(F32)).astype(BF)
-    out_ref[...] = jnp.broadcast_to(total[None], out_ref.shape)
+    out_ref[...] = (a_ref[...].astype(F32) + b_ref[...].astype(F32)).astype(BF)
+
+
+def sum_in_order(where_ref, refs, slots_ref):
+    own = where_ref[0] // CORES
+    for k, ref in enumerate(refs):
+        slots_ref[own ^ k] = ref[...].astype(F32)
+    return jnp.sum(slots_ref[...], 0)
 
 
 def exchange(pieces, axis):
     return lax.all_to_all(pieces, axis, 0, 0)
 
 
+def swap(value, mask):
+    pairs = [(i, i ^ mask) for i in range(lax.axis_size("kvh"))]
+    return lax.ppermute(value, "kvh", pairs)
+
+
 def parts_kvh(value):
-    size = lax.axis_size("kvh")
-    other = lax.ppermute(value, "kvh", [(i, i ^ 1) for i in range(size)])
-    both = call(add_kernel, bf(size // CORES, *value.shape), 2)(value, other)
-    columns = [list(range(core, size, CORES)) for core in range(CORES)]
-    return lax.all_to_all(both, "kvh", 0, 0, axis_index_groups=columns)
+    both = call(add_kernel, bf(*value.shape), 2)(value, swap(value, 1))
+    return [both] + [swap(both, k * CORES) for k in (1, 2, 3)]
 
 
 def shards(
@@ -240,6 +260,7 @@
 ):
     requests, heads, size = queries.shape
     seq = lax.axis_size("seq")
+    group = lax.axis_index("kvh").reshape(1)
     rows = requests * heads // seq
     width = residual.shape[1]
     halves = seq // requests
@@ -266,7 +287,7 @@
             pltpu.VMEM(cache, BF),
             pltpu.VMEM((requests, width), BF),
             pltpu.VMEM((width // LANES, LANES), BF),
-            DMA((8,)),
+            DMA((10,)),
         ],
         smem=(0,),
         hbm=range(1, 12),
@@ -292,14 +313,18 @@
         2,
         scratch=[pltpu.VMEM((requests * heads, size), F32)],
     )(exchange(merged, "seq"), out_weight)
-    middle, pieces = call(
+    middle, pieces, attended = call(
         gate_up_kernel,
-        (bf(requests, width), bf(seq, depth, LANES)),
-        5,
+        (bf(requests, width), bf(seq, depth, LANES), bf(requests, heads * size)),
+        10,
         scratch=[
             pltpu.VMEM((seq * depth, LANES), F32),
+            pltpu.VMEM((4, requests, width), F32),
+            DMA((1,)),
         ],
-    )(parts_kvh(projected), residual, gain, gate_weight, up_weight)
+        smem=(0,),
+        hbm_out=(2,),
+    )(group, *parts_kvh(projected), residual, gain, gate_weight, up_weight, attended)
     hidden = call(lambda *refs: hidden_kernel(blocks, *refs), bf(seq, thin, LANES), 1)(
         exchange(pieces, "seq")
     )
@@ -309,7 +334,13 @@
         2,
         scratch=[pltpu.VMEM((seq * thin, LANES), F32)],
     )(exchange(hidden, "seq"), down_weight)
-    updated = call(finish_kernel, bf(requests, width), 2)(parts_kvh(down), middle)
+    updated = call(
+        finish_kernel,
+        bf(requests, width),
+        6,
+        scratch=[pltpu.VMEM((4, requests, width), F32)],
+        smem=(0,),
+    )(group, *parts_kvh(down), middle)
     return (updated, attended)
 
 

time: 91.5 us -> 90 us (0.984)
  blocking collectives: 75.7 us -> 60.1 us
  starting transfers between devices: 7.32 us -> 14 us
  waiting for transfers between devices: 1.68 us -> 6.98 us
  local copies, waits for them, and re-layouts: 0.02 us -> 2.66 us
    all_to_all x2 -> x0, blocking collectives: 15.3 us -> none  [parts_kvh(): return lax.all_to_all(both, 'kvh', 0, 0, axis_index_groups=columns)]
    ppermute x2 -> x8, starting transfers between devices: 7.32 us -> 14 us  [swap(): return lax.ppermute(value, 'kvh', pairs)]
    ppermute x2 -> x8, waiting for transfers between devices: 1.68 us -> 6.98 us  [swap(): return lax.ppermute(value, 'kvh', pairs)]
    unnamed x8 -> x12, local copies, waits for them, and re-layouts: 0.02 us -> 2.66 us
  transfers between devices with their start and end apart: 2 -> 8, of which waited for: 2 -> 6; matrix products, arithmetic and copies ran while one was open for 0% -> 0% of each run, Pallas kernels for 0% -> 0%
where the time goes in v5:
time: 90 us; the launch traced here: 89.8 us
  blocking collectives  60.1 us (67%)
  starting transfers between devices  14 us (16%)
  waiting for transfers between devices  6.98 us (8%)
  Pallas kernels  5.31 us (6%)
  local copies, waits for them, and re-layouts  2.66 us (3%)
    all_to_all x4, blocking collectives, exchange(): return lax.all_to_all(pieces, axis, 0, 0)  60.1 us
    ppermute x8, starting transfers between devices, swap(): return lax.ppermute(value, 'kvh', pairs)  14 us
    ppermute x8, waiting for transfers between devices, swap(): return lax.ppermute(value, 'kvh', pairs)  6.98 us
    pallas_call x9, Pallas kernels, run(): kernel(*[pltpu.with_memory_space_constraint(arg, pltpu.HBM) if i in hbm e...  5.31 us
    unnamed x12, local copies, waits for them, and re-layouts  2.66 us
  transfers between devices with their start and end apart: 8, of which 6 were waited for; matrix products, arithmetic and copies ran while one was open for 0% of the time, Pallas kernels for 0%

profile of v5, /device:TPU:1, one launch (start us, length us, event | category | flops | bytes accessed | tf_op | source)
XLA Modules:
  0.0 89.8 jit_solution(2429261343679794124)
XLA Ops:
  0.6 0.0 copy-start.3
  0.6 0.0 copy-start.1
  0.7 2.2 %shard_map.131 = (bf16[16,16,256]{2,1,0:T(8,128)(2,1)S(1)}, bf16[16,512]{1,0:T(8,128)(2,1)S(1)}, f32[1,512]{1,0:T(1,128)S(1)}) custom-call(s32[1]{0:T(128)} %bitcast.1.where_ref, s32[16]{0:T(128)} %refs_0_.1, bf16[16,16,128]{2,1,0:T(8,128)(2,1)} %refs_1_.1, bf16[16,128]{1,0:T(8,128)(2,1)} %bitcast.11, bf16[16,128,128]{2,1,0:T(8,128)(2,1)} %bitcast.9, ...), custom_call_target="tpu_custom_call" | custom-call | tf_op jit(solution)/shard_map/pallas_call | solution.py:33
  2.9 0.0 copy-start.4
  2.9 20.8 %all_to_all.20.got_ref = bf16[32,8,256]{2,1,0:T(8,128)(2,1)S(1)} all-to-all(bf16[32,8,256]{2,1,0:T(8,128)(2,1)S(1)} %bitcast.8), channel_id=1, replica_groups=mesh['kvh'=8,'seq'=32] {'seq'}, dimensions={0} | all-to-all | bytes 262144 | tf_op jit(solution)/shard_map/all_to_all | solution.py:234
  23.7 0.2 shard_map.132
  23.9 12.4 %all_to_all.21.got_ref = bf16[32,8,128]{2,1,0:T(8,128)(2,1)S(1)} all-to-all(bf16[32,8,128]{2,1,0:T(8,128)(2,1)S(1)} %shard_map.132), channel_id=1, replica_groups=mesh['kvh'=8,'seq'=32] {'seq'}, dimensions={0} | all-to-all | bytes 131072 | tf_op jit(solution)/shard_map/all_to_all | solution.py:234
  36.3 0.0 copy-done.3
  36.3 0.4 shard_map.133
  36.7 3.3 %collective-permute-start = (bf16[16,512]{1,0:T(8,128)(2,1)S(1)}, bf16[16,512]{1,0:T(8,128)(2,1)S(1)}, u32[]{:S(2)}, u32[]{:S(2)}) collective-permute-start(bf16[16,512]{1,0:T(8,128)(2,1)S(1)} %get-tuple-element.11.a_ref), channel_id=1, source_target_pairs={{0,32},{32,0},{64,96},{96,64},{128,160},{160,128},{192,224},{224,1... | collective-permute-start | bytes 49160 | tf_op jit(solution)/shard_map/ppermute | solution.py:239
  40.0 0.0 copy-done.4
  40.0 0.8 collective-permute-done.b_ref
  40.8 2.7 %collective-permute-start.3 = (bf16[16,512]{1,0:T(8,128)(2,1)S(1)}, bf16[16,512]{1,0:T(8,128)(2,1)S(1)}, u32[]{:S(2)}, u32[]{:S(2)}) collective-permute-start(bf16[16,512]{1,0:T(8,128)(2,1)S(1)} %shard_map.134.p0_ref), channel_id=1, source_target_pairs={{0,192},{32,224},{64,128},{96,160},{128,64},{160,96},{192,0},{224,... | collective-permute-start | bytes 49160 | tf_op jit(solution)/shard_map/ppermute | solution.py:239
  43.6 0.3 collective-permute-start.2
  43.9 0.3 collective-permute-start.1
  44.2 0.5 collective-permute-done.3.p3_ref
  44.7 3.0 %collective-permute-done.2.p2_ref = bf16[16,512]{1,0:T(8,128)(2,1)S(1)} collective-permute-done((bf16[16,512]{1,0:T(8,128)(2,1)S(1)}, bf16[16,512]{1,0:T(8,128)(2,1)S(1)}, u32[]{:S(2)}, u32[]{:S(2)}) %collective-permute-start.2) | collective-permute-done | bytes 16416 | tf_op jit(solution)/shard_map/ppermute | solution.py:239
  47.7 0.0 collective-permute-done.1.p1_ref
  47.7 0.0 copy-done.1
  47.7 0.0 copy-start.2
  47.7 2.0 %copy-done.2 = bf16[512,3328]{1,0:T(8,128)(2,1)S(1)} copy-done((bf16[512,3328]{1,0:T(8,128)(2,1)S(1)}, bf16[512,3328]{1,0:T(8,128)(2,1)}, u32[]{:S(2)}) %copy-start.2) | copy-done | bytes 3407896
  49.6 0.0 copy-start.5
  49.6 0.7 copy-done.5
  50.3 0.0 copy-start
  50.3 1.1 %shard_map.135 = (bf16[16,512]{1,0:T(8,128)(2,1)S(1)}, bf16[32,32,128]{2,1,0:T(8,128)(2,1)S(1)}, bf16[16,2048]{1,0:T(8,128)(2,1)}) custom-call(s32[1]{0:T(128)} %bitcast.where_ref, bf16[16,512]{1,0:T(8,128)(2,1)S(1)} %shard_map.134.p0_ref, bf16[16,512]{1,0:T(8,128)(2,1)S(1)} %collective-permute-done.1.p1_ref, ...), custom_call_target="tpu_custom_call" | custom-call | tf_op jit(solution)/shard_map/pallas_call | solution.py:33
  51.5 12.6 %all_to_all.22.refs_0_ = bf16[32,32,128]{2,1,0:T(8,128)(2,1)S(1)} all-to-all(bf16[32,32,128]{2,1,0:T(8,128)(2,1)S(1)} %get-tuple-element.15), channel_id=1, replica_groups=mesh['kvh'=8,'seq'=32] {'seq'}, dimensions={0} | all-to-all | bytes 524288 | tf_op jit(solution)/shard_map/all_to_all | solution.py:234
  64.1 0.2 shard_map.136
  64.3 14.3 %all_to_all.23.got_ref = bf16[32,16,128]{2,1,0:T(8,128)(2,1)S(1)} all-to-all(bf16[32,16,128]{2,1,0:T(8,128)(2,1)S(1)} %shard_map.136), channel_id=1, replica_groups=mesh['kvh'=8,'seq'=32] {'seq'}, dimensions={0} | all-to-all | bytes 262144 | tf_op jit(solution)/shard_map/all_to_all | solution.py:234
  78.6 0.0 copy-done
  78.6 0.6 shard_map.137.a_ref
  79.1 4.0 %collective-permute-start.4 = (bf16[16,512]{1,0:T(8,128)(2,1)S(1)}, bf16[16,512]{1,0:T(8,128)(2,1)S(1)}, u32[]{:S(2)}, u32[]{:S(2)}) collective-permute-start(bf16[16,512]{1,0:T(8,128)(2,1)S(1)} %shard_map.137.a_ref), channel_id=1, source_target_pairs={{0,32},{32,0},{64,96},{96,64},{128,160},{160,128},{192,224},{224,1... | collective-permute-start | bytes 49160 | tf_op jit(solution)/shard_map/ppermute | solution.py:239
  83.2 0.8 collective-permute-done.4.b_ref
  84.0 1.0 %collective-permute-start.7 = (bf16[16,512]{1,0:T(8,128)(2,1)S(1)}, bf16[16,512]{1,0:T(8,128)(2,1)S(1)}, u32[]{:S(2)}, u32[]{:S(2)}) collective-permute-start(bf16[16,512]{1,0:T(8,128)(2,1)S(1)} %shard_map.138.p0_ref), channel_id=1, source_target_pairs={{0,192},{32,224},{64,128},{96,160},{128,64},{160,96},{192,0},{224,... | collective-permute-start | bytes 49160 | tf_op jit(solution)/shard_map/ppermute | solution.py:239
  85.1 0.8 collective-permute-start.6
  85.8 1.4 %collective-permute-start.5 = (bf16[16,512]{1,0:T(8,128)(2,1)S(1)}, bf16[16,512]{1,0:T(8,128)(2,1)S(1)}, u32[]{:S(2)}, u32[]{:S(2)}) collective-permute-start(bf16[16,512]{1,0:T(8,128)(2,1)S(1)} %shard_map.138.p0_ref), channel_id=1, source_target_pairs={{0,64},{32,96},{64,0},{96,32},{128,192},{160,224},{192,128},{224,1... | collective-permute-start | bytes 49160 | tf_op jit(solution)/shard_map/ppermute | solution.py:239
  87.3 0.5 collective-permute-done.7.p3_ref
  87.8 1.3 %collective-permute-done.6.p2_ref = bf16[16,512]{1,0:T(8,128)(2,1)S(1)} collective-permute-done((bf16[16,512]{1,0:T(8,128)(2,1)S(1)}, bf16[16,512]{1,0:T(8,128)(2,1)S(1)}, u32[]{:S(2)}, u32[]{:S(2)}) %collective-permute-start.6) | collective-permute-done | bytes 16416 | tf_op jit(solution)/shard_map/ppermute | solution.py:239
  89.1 0.0 collective-permute-done.5.p1_ref
  89.2 0.6 shard_map.139
  (2 shorter events, 0.0 us)
Async XLA Ops:
  0.6 35.7 %copy-start.3 = (bf16[2048,512]{1,0:T(8,128)(2,1)S(1)}, bf16[2048,512]{1,0:T(8,128)(2,1)}, u32[]{:S(2)}) copy-start(bf16[2048,512]{1,0:T(8,128)(2,1)} %weight_ref.2) | copy-start | bytes 6291460
  0.6 47.0 %copy-start.1 = (bf16[512,3328]{1,0:T(8,128)(2,1)S(1)}, bf16[512,3328]{1,0:T(8,128)(2,1)}, u32[]{:S(2)}) copy-start(bf16[512,3328]{1,0:T(8,128)(2,1)} %gate_ref.1) | copy-start | bytes 10223620
  2.9 37.1 %copy-start.4 = (f32[1,512]{1,0:T(1,128)}, f32[1,512]{1,0:T(1,128)S(1)}, u32[]{:S(2)}) copy-start(f32[1,512]{1,0:T(1,128)S(1)} %get-tuple-element.13.gain_ref) | copy-start | bytes 6148
  36.7 4.1 %collective-permute-start = (bf16[16,512]{1,0:T(8,128)(2,1)S(1)}, bf16[16,512]{1,0:T(8,128)(2,1)S(1)}, u32[]{:S(2)}, u32[]{:S(2)}) collective-permute-start(bf16[16,512]{1,0:T(8,128)(2,1)S(1)} %get-tuple-element.11.a_ref), channel_id=1, source_target_pairs={{0,32},{32,0},{64,96},{96,64},{128,160},{160,128},{192,224},{224,1... | collective-permute-start | bytes 49160 | tf_op jit(solution)/shard_map/ppermute | solution.py:239
  40.8 3.9 %collective-permute-start.3 = (bf16[16,512]{1,0:T(8,128)(2,1)S(1)}, bf16[16,512]{1,0:T(8,128)(2,1)S(1)}, u32[]{:S(2)}, u32[]{:S(2)}) collective-permute-start(bf16[16,512]{1,0:T(8,128)(2,1)S(1)} %shard_map.134.p0_ref), channel_id=1, source_target_pairs={{0,192},{32,224},{64,128},{96,160},{128,64},{160,96},{192,0},{224,... | collective-permute-start | bytes 49160 | tf_op jit(solution)/shard_map/ppermute | solution.py:239
  43.6 4.1 %collective-permute-start.2 = (bf16[16,512]{1,0:T(8,128)(2,1)S(1)}, bf16[16,512]{1,0:T(8,128)(2,1)S(1)}, u32[]{:S(2)}, u32[]{:S(2)}) collective-permute-start(bf16[16,512]{1,0:T(8,128)(2,1)S(1)} %shard_map.134.p0_ref), channel_id=1, source_target_pairs={{0,128},{32,160},{64,192},{96,224},{128,0},{160,32},{192,64},{224,... | collective-permute-start | bytes 49160 | tf_op jit(solution)/shard_map/ppermute | solution.py:239
  43.9 3.7 %collective-permute-start.1 = (bf16[16,512]{1,0:T(8,128)(2,1)S(1)}, bf16[16,512]{1,0:T(8,128)(2,1)S(1)}, u32[]{:S(2)}, u32[]{:S(2)}) collective-permute-start(bf16[16,512]{1,0:T(8,128)(2,1)S(1)} %shard_map.134.p0_ref), channel_id=1, source_target_pairs={{0,64},{32,96},{64,0},{96,32},{128,192},{160,224},{192,128},{224,1... | collective-permute-start | bytes 49160 | tf_op jit(solution)/shard_map/ppermute | solution.py:239
  47.7 2.0 %copy-start.2 = (bf16[512,3328]{1,0:T(8,128)(2,1)S(1)}, bf16[512,3328]{1,0:T(8,128)(2,1)}, u32[]{:S(2)}) copy-start(bf16[512,3328]{1,0:T(8,128)(2,1)} %up_ref.1) | copy-start | bytes 10223620
  49.6 0.7 copy-start.5
  50.3 28.3 %copy-start = (bf16[3328,512]{1,0:T(8,128)(2,1)S(1)}, bf16[3328,512]{1,0:T(8,128)(2,1)}, u32[]{:S(2)}) copy-start(bf16[3328,512]{1,0:T(8,128)(2,1)} %weight_ref.3) | copy-start | bytes 10223620
  79.1 4.9 %collective-permute-start.4 = (bf16[16,512]{1,0:T(8,128)(2,1)S(1)}, bf16[16,512]{1,0:T(8,128)(2,1)S(1)}, u32[]{:S(2)}, u32[]{:S(2)}) collective-permute-start(bf16[16,512]{1,0:T(8,128)(2,1)S(1)} %shard_map.137.a_ref), channel_id=1, source_target_pairs={{0,32},{32,0},{64,96},{96,64},{128,160},{160,128},{192,224},{224,1... | collective-permute-start | bytes 49160 | tf_op jit(solution)/shard_map/ppermute | solution.py:239
  84.0 3.8 %collective-permute-start.7 = (bf16[16,512]{1,0:T(8,128)(2,1)S(1)}, bf16[16,512]{1,0:T(8,128)(2,1)S(1)}, u32[]{:S(2)}, u32[]{:S(2)}) collective-permute-start(bf16[16,512]{1,0:T(8,128)(2,1)S(1)} %shard_map.138.p0_ref), channel_id=1, source_target_pairs={{0,192},{32,224},{64,128},{96,160},{128,64},{160,96},{192,0},{224,... | collective-permute-start | bytes 49160 | tf_op jit(solution)/shard_map/ppermute | solution.py:239
  85.1 4.1 %collective-permute-start.6 = (bf16[16,512]{1,0:T(8,128)(2,1)S(1)}, bf16[16,512]{1,0:T(8,128)(2,1)S(1)}, u32[]{:S(2)}, u32[]{:S(2)}) collective-permute-start(bf16[16,512]{1,0:T(8,128)(2,1)S(1)} %shard_map.138.p0_ref), channel_id=1, source_target_pairs={{0,128},{32,160},{64,192},{96,224},{128,0},{160,32},{192,64},{224,... | collective-permute-start | bytes 49160 | tf_op jit(solution)/shard_map/ppermute | solution.py:239
  85.8 3.3 %collective-permute-start.5 = (bf16[16,512]{1,0:T(8,128)(2,1)S(1)}, bf16[16,512]{1,0:T(8,128)(2,1)S(1)}, u32[]{:S(2)}, u32[]{:S(2)}) collective-permute-start(bf16[16,512]{1,0:T(8,128)(2,1)S(1)} %shard_map.138.p0_ref), channel_id=1, source_target_pairs={{0,64},{32,96},{64,0},{96,32},{128,192},{160,224},{192,128},{224,1... | collective-permute-start | bytes 49160 | tf_op jit(solution)/shard_map/ppermute | solution.py:239

commit v6 on v5

--- a/solution.py
+++ b/solution.py
@@ -76,7 +76,7 @@
     return copies
 
 
-def attention_kernel(where_ref, *refs):
+def attention_kernel(where_ref, group_ref, *refs):
     sources, refs = refs[:8], refs[-12:]
     out_ref, kept_ref, row_ref = refs[:3]
     targets, sems = refs[3:11], refs[11]
@@ -277,7 +277,7 @@
             bf(requests, width),
             jax.ShapeDtypeStruct((1, width), F32),
         ),
-        12,
+        13,
         scratch=[
             pltpu.SMEM((requests,), jnp.int32),
             pltpu.VMEM((requests, heads, size), BF),
@@ -289,10 +289,11 @@
             pltpu.VMEM((width // LANES, LANES), BF),
             DMA((10,)),
         ],
-        smem=(0,),
-        hbm=range(1, 12),
+        smem=(0, 1),
+        hbm=range(2, 13),
     )(
         where,
+        group,
         lengths,
         queries,
         token_keys.reshape(requests, size),

time: 90 us -> 87.5 us (0.972)
  local copies, waits for them, and re-layouts: 2.66 us -> 0.02 us
    unnamed x12 -> x8, local copies, waits for them, and re-layouts: 2.66 us -> 0.02 us
where the time goes in v6:
time: 87.5 us; the launch traced here: 87.3 us
  blocking collectives  60.3 us (69%)
  starting transfers between devices  14 us (16%)
  waiting for transfers between devices  6.97 us (8%)
  Pallas kernels  5.33 us (6%)
    all_to_all x4, blocking collectives, exchange(): return lax.all_to_all(pieces, axis, 0, 0)  60.3 us
    ppermute x8, starting transfers between devices, swap(): return lax.ppermute(value, 'kvh', pairs)  14 us
    ppermute x8, waiting for transfers between devices, swap(): return lax.ppermute(value, 'kvh', pairs)  6.97 us
    pallas_call x9, Pallas kernels, run(): kernel(*[pltpu.with_memory_space_constraint(arg, pltpu.HBM) if i in hbm e...  5.33 us
  transfers between devices with their start and end apart: 8, of which 6 were waited for; matrix products, arithmetic and copies ran while one was open for 0% of the time, Pallas kernels for 0%

profile of v6, /device:TPU:1, one launch (start us, length us, event | category | flops | bytes accessed | tf_op | source)
XLA Modules:
  0.0 87.3 jit_solution(7175930757357439786)
XLA Ops:
  0.6 0.0 copy-start.3
  0.6 0.0 copy-start.1
  0.7 0.0 copy-start.2
  0.7 2.2 %shard_map.131 = (bf16[16,16,256]{2,1,0:T(8,128)(2,1)S(1)}, bf16[16,512]{1,0:T(8,128)(2,1)S(1)}, f32[1,512]{1,0:T(1,128)S(1)}) custom-call(s32[1]{0:T(128)} %bitcast.1.where_ref, s32[1]{0:T(128)} %bitcast.group_ref.where_ref, s32[16]{0:T(128)} %refs_0_.1, bf16[16,16,128]{2,1,0:T(8,128)(2,1)} %refs_1_.1, bf16[16,128]{1,0:T(8,128)(2,1)} %bitcast.11, ...), custom_call_target="tpu_custom_call" | custom-call | tf_op jit(solution)/shard_map/pallas_call | solution.py:33
  2.9 20.9 %all_to_all.20.got_ref = bf16[32,8,256]{2,1,0:T(8,128)(2,1)S(1)} all-to-all(bf16[32,8,256]{2,1,0:T(8,128)(2,1)S(1)} %bitcast.8), channel_id=1, replica_groups=mesh['kvh'=8,'seq'=32] {'seq'}, dimensions={0} | all-to-all | bytes 262144 | tf_op jit(solution)/shard_map/all_to_all | solution.py:234
  23.8 0.2 shard_map.132
  24.1 12.4 %all_to_all.21.got_ref = bf16[32,8,128]{2,1,0:T(8,128)(2,1)S(1)} all-to-all(bf16[32,8,128]{2,1,0:T(8,128)(2,1)S(1)} %shard_map.132), channel_id=1, replica_groups=mesh['kvh'=8,'seq'=32] {'seq'}, dimensions={0} | all-to-all | bytes 131072 | tf_op jit(solution)/shard_map/all_to_all | solution.py:234
  36.4 0.0 copy-done.3
  36.5 0.4 shard_map.133
  36.8 3.3 %collective-permute-start = (bf16[16,512]{1,0:T(8,128)(2,1)S(1)}, bf16[16,512]{1,0:T(8,128)(2,1)S(1)}, u32[]{:S(2)}, u32[]{:S(2)}) collective-permute-start(bf16[16,512]{1,0:T(8,128)(2,1)S(1)} %get-tuple-element.11.a_ref), channel_id=1, source_target_pairs={{0,32},{32,0},{64,96},{96,64},{128,160},{160,128},{192,224},{224,1... | collective-permute-start | bytes 49160 | tf_op jit(solution)/shard_map/ppermute | solution.py:239
  40.1 0.8 collective-permute-done.b_ref
  41.0 2.7 %collective-permute-start.3 = (bf16[16,512]{1,0:T(8,128)(2,1)S(1)}, bf16[16,512]{1,0:T(8,128)(2,1)S(1)}, u32[]{:S(2)}, u32[]{:S(2)}) collective-permute-start(bf16[16,512]{1,0:T(8,128)(2,1)S(1)} %shard_map.134.p0_ref), channel_id=1, source_target_pairs={{0,192},{32,224},{64,128},{96,160},{128,64},{160,96},{192,0},{224,... | collective-permute-start | bytes 49160 | tf_op jit(solution)/shard_map/ppermute | solution.py:239
  43.7 0.3 collective-permute-start.2
  44.0 0.3 collective-permute-start.1
  44.4 0.5 collective-permute-done.3.p3_ref
  44.8 3.0 %collective-permute-done.2.p2_ref = bf16[16,512]{1,0:T(8,128)(2,1)S(1)} collective-permute-done((bf16[16,512]{1,0:T(8,128)(2,1)S(1)}, bf16[16,512]{1,0:T(8,128)(2,1)S(1)}, u32[]{:S(2)}, u32[]{:S(2)}) %collective-permute-start.2) | collective-permute-done | bytes 16416 | tf_op jit(solution)/shard_map/ppermute | solution.py:239
  47.8 0.0 collective-permute-done.1.p1_ref
  47.8 0.0 copy-done.1
  47.8 0.0 copy-done.2
  47.8 0.0 copy-start
  47.8 1.2 %shard_map.135 = (bf16[16,512]{1,0:T(8,128)(2,1)S(1)}, bf16[32,32,128]{2,1,0:T(8,128)(2,1)S(1)}, bf16[16,2048]{1,0:T(8,128)(2,1)}) custom-call(s32[1]{0:T(128)} %bitcast.group_ref.where_ref, bf16[16,512]{1,0:T(8,128)(2,1)S(1)} %shard_map.134.p0_ref, bf16[16,512]{1,0:T(8,128)(2,1)S(1)} %collective-permute-done.1.p1_ref, ...), custom_call_target="tpu_custom_call" | custom-call | tf_op jit(solution)/shard_map/pallas_call | solution.py:33
  49.0 12.6 %all_to_all.22.refs_0_ = bf16[32,32,128]{2,1,0:T(8,128)(2,1)S(1)} all-to-all(bf16[32,32,128]{2,1,0:T(8,128)(2,1)S(1)} %get-tuple-element.15), channel_id=1, replica_groups=mesh['kvh'=8,'seq'=32] {'seq'}, dimensions={0} | all-to-all | bytes 524288 | tf_op jit(solution)/shard_map/all_to_all | solution.py:234
  61.6 0.2 shard_map.136
  61.8 14.3 %all_to_all.23.got_ref = bf16[32,16,128]{2,1,0:T(8,128)(2,1)S(1)} all-to-all(bf16[32,16,128]{2,1,0:T(8,128)(2,1)S(1)} %shard_map.136), channel_id=1, replica_groups=mesh['kvh'=8,'seq'=32] {'seq'}, dimensions={0} | all-to-all | bytes 262144 | tf_op jit(solution)/shard_map/all_to_all | solution.py:234
  76.1 0.0 copy-done
  76.1 0.6 shard_map.137.a_ref
  76.6 4.0 %collective-permute-start.4 = (bf16[16,512]{1,0:T(8,128)(2,1)S(1)}, bf16[16,512]{1,0:T(8,128)(2,1)S(1)}, u32[]{:S(2)}, u32[]{:S(2)}) collective-permute-start(bf16[16,512]{1,0:T(8,128)(2,1)S(1)} %shard_map.137.a_ref), channel_id=1, source_target_pairs={{0,32},{32,0},{64,96},{96,64},{128,160},{160,128},{192,224},{224,1... | collective-permute-start | bytes 49160 | tf_op jit(solution)/shard_map/ppermute | solution.py:239
  80.7 0.8 collective-permute-done.4.b_ref
  81.5 1.0 %collective-permute-start.7 = (bf16[16,512]{1,0:T(8,128)(2,1)S(1)}, bf16[16,512]{1,0:T(8,128)(2,1)S(1)}, u32[]{:S(2)}, u32[]{:S(2)}) collective-permute-start(bf16[16,512]{1,0:T(8,128)(2,1)S(1)} %shard_map.138.p0_ref), channel_id=1, source_target_pairs={{0,192},{32,224},{64,128},{96,160},{128,64},{160,96},{192,0},{224,... | collective-permute-start | bytes 49160 | tf_op jit(solution)/shard_map/ppermute | solution.py:239
  82.6 0.8 collective-permute-start.6
  83.3 1.4 %collective-permute-start.5 = (bf16[16,512]{1,0:T(8,128)(2,1)S(1)}, bf16[16,512]{1,0:T(8,128)(2,1)S(1)}, u32[]{:S(2)}, u32[]{:S(2)}) collective-permute-start(bf16[16,512]{1,0:T(8,128)(2,1)S(1)} %shard_map.138.p0_ref), channel_id=1, source_target_pairs={{0,64},{32,96},{64,0},{96,32},{128,192},{160,224},{192,128},{224,1... | collective-permute-start | bytes 49160 | tf_op jit(solution)/shard_map/ppermute | solution.py:239
  84.8 0.5 collective-permute-done.7.p3_ref
  85.3 1.3 %collective-permute-done.6.p2_ref = bf16[16,512]{1,0:T(8,128)(2,1)S(1)} collective-permute-done((bf16[16,512]{1,0:T(8,128)(2,1)S(1)}, bf16[16,512]{1,0:T(8,128)(2,1)S(1)}, u32[]{:S(2)}, u32[]{:S(2)}) %collective-permute-start.6) | collective-permute-done | bytes 16416 | tf_op jit(solution)/shard_map/ppermute | solution.py:239
  86.7 0.0 collective-permute-done.5.p1_ref
  86.7 0.6 shard_map.139
  (2 shorter events, 0.0 us)
Async XLA Ops:
  0.6 35.8 %copy-start.3 = (bf16[2048,512]{1,0:T(8,128)(2,1)S(1)}, bf16[2048,512]{1,0:T(8,128)(2,1)}, u32[]{:S(2)}) copy-start(bf16[2048,512]{1,0:T(8,128)(2,1)} %weight_ref.2) | copy-start | bytes 6291460
  0.6 47.1 %copy-start.1 = (bf16[512,3328]{1,0:T(8,128)(2,1)S(1)}, bf16[512,3328]{1,0:T(8,128)(2,1)}, u32[]{:S(2)}) copy-start(bf16[512,3328]{1,0:T(8,128)(2,1)} %gate_ref.1) | copy-start | bytes 10223620
  0.7 47.1 %copy-start.2 = (bf16[512,3328]{1,0:T(8,128)(2,1)S(1)}, bf16[512,3328]{1,0:T(8,128)(2,1)}, u32[]{:S(2)}) copy-start(bf16[512,3328]{1,0:T(8,128)(2,1)} %up_ref.1) | copy-start | bytes 10223620
  36.8 4.1 %collective-permute-start = (bf16[16,512]{1,0:T(8,128)(2,1)S(1)}, bf16[16,512]{1,0:T(8,128)(2,1)S(1)}, u32[]{:S(2)}, u32[]{:S(2)}) collective-permute-start(bf16[16,512]{1,0:T(8,128)(2,1)S(1)} %get-tuple-element.11.a_ref), channel_id=1, source_target_pairs={{0,32},{32,0},{64,96},{96,64},{128,160},{160,128},{192,224},{224,1... | collective-permute-start | bytes 49160 | tf_op jit(solution)/shard_map/ppermute | solution.py:239
  41.0 3.9 %collective-permute-start.3 = (bf16[16,512]{1,0:T(8,128)(2,1)S(1)}, bf16[16,512]{1,0:T(8,128)(2,1)S(1)}, u32[]{:S(2)}, u32[]{:S(2)}) collective-permute-start(bf16[16,512]{1,0:T(8,128)(2,1)S(1)} %shard_map.134.p0_ref), channel_id=1, source_target_pairs={{0,192},{32,224},{64,128},{96,160},{128,64},{160,96},{192,0},{224,... | collective-permute-start | bytes 49160 | tf_op jit(solution)/shard_map/ppermute | solution.py:239
  43.7 4.1 %collective-permute-start.2 = (bf16[16,512]{1,0:T(8,128)(2,1)S(1)}, bf16[16,512]{1,0:T(8,128)(2,1)S(1)}, u32[]{:S(2)}, u32[]{:S(2)}) collective-permute-start(bf16[16,512]{1,0:T(8,128)(2,1)S(1)} %shard_map.134.p0_ref), channel_id=1, source_target_pairs={{0,128},{32,160},{64,192},{96,224},{128,0},{160,32},{192,64},{224,... | collective-permute-start | bytes 49160 | tf_op jit(solution)/shard_map/ppermute | solution.py:239
  44.0 3.7 %collective-permute-start.1 = (bf16[16,512]{1,0:T(8,128)(2,1)S(1)}, bf16[16,512]{1,0:T(8,128)(2,1)S(1)}, u32[]{:S(2)}, u32[]{:S(2)}) collective-permute-start(bf16[16,512]{1,0:T(8,128)(2,1)S(1)} %shard_map.134.p0_ref), channel_id=1, source_target_pairs={{0,64},{32,96},{64,0},{96,32},{128,192},{160,224},{192,128},{224,1... | collective-permute-start | bytes 49160 | tf_op jit(solution)/shard_map/ppermute | solution.py:239
  47.8 28.3 %copy-start = (bf16[3328,512]{1,0:T(8,128)(2,1)S(1)}, bf16[3328,512]{1,0:T(8,128)(2,1)}, u32[]{:S(2)}) copy-start(bf16[3328,512]{1,0:T(8,128)(2,1)} %weight_ref.3) | copy-start | bytes 10223620
  76.6 4.9 %collective-permute-start.4 = (bf16[16,512]{1,0:T(8,128)(2,1)S(1)}, bf16[16,512]{1,0:T(8,128)(2,1)S(1)}, u32[]{:S(2)}, u32[]{:S(2)}) collective-permute-start(bf16[16,512]{1,0:T(8,128)(2,1)S(1)} %shard_map.137.a_ref), channel_id=1, source_target_pairs={{0,32},{32,0},{64,96},{96,64},{128,160},{160,128},{192,224},{224,1... | collective-permute-start | bytes 49160 | tf_op jit(solution)/shard_map/ppermute | solution.py:239
  81.5 3.8 %collective-permute-start.7 = (bf16[16,512]{1,0:T(8,128)(2,1)S(1)}, bf16[16,512]{1,0:T(8,128)(2,1)S(1)}, u32[]{:S(2)}, u32[]{:S(2)}) collective-permute-start(bf16[16,512]{1,0:T(8,128)(2,1)S(1)} %shard_map.138.p0_ref), channel_id=1, source_target_pairs={{0,192},{32,224},{64,128},{96,160},{128,64},{160,96},{192,0},{224,... | collective-permute-start | bytes 49160 | tf_op jit(solution)/shard_map/ppermute | solution.py:239
  82.6 4.1 %collective-permute-start.6 = (bf16[16,512]{1,0:T(8,128)(2,1)S(1)}, bf16[16,512]{1,0:T(8,128)(2,1)S(1)}, u32[]{:S(2)}, u32[]{:S(2)}) collective-permute-start(bf16[16,512]{1,0:T(8,128)(2,1)S(1)} %shard_map.138.p0_ref), channel_id=1, source_target_pairs={{0,128},{32,160},{64,192},{96,224},{128,0},{160,32},{192,64},{224,... | collective-permute-start | bytes 49160 | tf_op jit(solution)/shard_map/ppermute | solution.py:239
  83.3 3.3 %collective-permute-start.5 = (bf16[16,512]{1,0:T(8,128)(2,1)S(1)}, bf16[16,512]{1,0:T(8,128)(2,1)S(1)}, u32[]{:S(2)}, u32[]{:S(2)}) collective-permute-start(bf16[16,512]{1,0:T(8,128)(2,1)S(1)} %shard_map.138.p0_ref), channel_id=1, source_target_pairs={{0,64},{32,96},{64,0},{96,32},{128,192},{160,224},{192,128},{224,1... | collective-permute-start | bytes 49160 | tf_op jit(solution)/shard_map/ppermute | solution.py:239
